TPU v7x, 512 devices: a whole 4x8x8 slice. The times are simulated.
512 devices in a mesh: span: 32 (over z, x), sub: 16 (over y, core).
Axes of the slice: x: 4, y: 8, z: 8, core: 2. Of those that a mesh axis runs over, the one named last changes fastest.
Arguments:
- stress: bfloat16 [512, 768, 128], P(('span', 'sub')), may hold values from -6 to 6
- history: float32 [8, 512, 768], P(None, ('span', 'sub')), may hold values from -6 to 6
- retard: float32 [8], replicated, may hold values from 0.3 to 30
- compliance: float32 [8], replicated, may hold values from 0.2 to 2
- micro: float32 [512, 768], P(('span', 'sub')), may hold values from 0.5 to 5
- lengths: int32 [512], P(('span', 'sub')), may hold values from 1 to 768, 131072 in all
- multiplier_index: int32 [512, 768], P(('span', 'sub')), may hold values from 0 to 131071, as said below
- dual_block: bfloat16 [512, 768, 768], P(('span', 'sub')), may hold values from -1 to 4, as said below
- corner_map: bfloat16 [512, 768, 128], P(('span', 'sub')), may hold values from -0.21875 to 0.21875
- coarse_stiffness_inverse: float32 [32, 128, 128], P('span'), may hold values from -1 to 4, as said below
Outputs:
- solution: float32 [131072, 128], P(('span', 'sub'))
- residual: float32 [131072, 128], P(('span', 'sub'))
Inputs may be any that keep to these rules, and one draw needn't show every extreme that they name: `multiplier_index`: each slot of a subdomain names a multiplier held by its own device or by the device of the same sub index in one of the two neighbouring spans; multipliers 0 and 131071 are named in every draw. `dual_block`: each block is symmetric with a diagonal between 1 and 4. `coarse_stiffness_inverse`: each span's matrix is symmetric with a diagonal between 1 and 4.
All inputs are finite; a program needn't handle non-finite values. No bound on the sum of `lengths` on one device may be relied on, other than what follows from the above.
Results may differ from a plain program's by a relative error of at most 0.024.
Values may be sent and summed in bfloat16 or wider, within the bound.
A program may use at most 64 MiB of HBM per device.

v0:
```python
import jax
import jax.numpy as jnp
from jax import lax
from jax.sharding import PartitionSpec as P

ITERS = 2


def from_behind(shard, axis, by):
    size = lax.axis_size(axis)
    pairs = [(i, i + by) for i in range(size) if 0 <= i + by < size]
    return lax.ppermute(shard, axis, pairs)


def padded(shard, sides, width):
    for axis, dim in sides:
        size, length = (lax.axis_size(axis), shard.shape[dim])
        up = [(i, (i + 1) % size) for i in range(size - 1)]
        down = [(j, i) for i, j in up]
        last = lax.slice_in_dim(shard, length - width, length, axis=dim)
        leading = lax.slice_in_dim(shard, 0, width, axis=dim)
        before = lax.ppermute(last, axis, up)
        after = lax.ppermute(leading, axis, down)
        shard = jnp.concatenate([before, shard, after], axis=dim)
    return shard


def column_sums(left, right):
    return jnp.sum(left * right, axis=0)


def on_device(
    stress,
    history,
    retard,
    compliance,
    micro,
    lengths,
    multiplier_index,
    dual_block,
    corner_map,
    coarse_stiffness_inverse,
):
    sub_count = dual_block.shape[0]
    width = dual_block.shape[1]
    loads = stress.shape[2]
    owned = sub_count * width // 3
    groups = lax.axis_size("sub")
    here = lax.axis_index("span")
    live = (jnp.arange(width)[None, :] < lengths[:, None]).astype(jnp.float32)
    owner_dev = multiplier_index // owned
    window_pos = ((owner_dev // groups - here + 1) * owned + multiplier_index % owned).reshape(-1)
    weight_k = 1.0 - jnp.exp(-1.0 / retard)
    creep = jnp.sum(weight_k * compliance)
    past = jnp.sum(weight_k[:, None, None] * history, axis=0)
    relaxed = micro / (1.0 + micro)
    load = (
        (creep + 0.5 * relaxed[:, :, None]) * stress.astype(jnp.float32) - past[:, :, None]
    ) * live[:, :, None]

    def assemble(local):
        window = (
            jnp.zeros((3 * owned, loads), jnp.float32).at[window_pos].add(local.reshape(-1, loads))
        )
        from_next = from_behind(window[:owned], "span", -1)
        from_prev = from_behind(window[2 * owned :], "span", 1)
        return window[owned : 2 * owned] + from_next + from_prev

    kernel = coarse_stiffness_inverse[0]
    rhs = assemble(load)
    solution = jnp.zeros_like(rhs)
    residual = rhs
    direction = rhs
    norm_now = lax.psum(column_sums(residual, residual), ("span", "sub"))
    for step in range(ITERS):
        narrow = direction.astype(jnp.bfloat16)
        apply_window = padded(narrow, (("span", 0),), owned)
        gathered = (
            apply_window[window_pos].reshape(sub_count, width, loads).astype(jnp.float32)
            * live[:, :, None]
        ).astype(jnp.bfloat16)
        apply_local = jnp.einsum(
            "smn,snr->smr", dual_block, gathered, preferred_element_type=jnp.float32
        )
        corner_part = jnp.einsum(
            "smc,smr->cr", corner_map, gathered, preferred_element_type=jnp.float32
        )
        corner_residual = lax.psum(corner_part.astype(jnp.bfloat16), "sub").astype(jnp.float32)
        corner_update = jnp.dot(kernel, corner_residual, precision=lax.Precision.HIGHEST)
        spread_corners = jnp.einsum(
            "smc,cr->smr",
            corner_map,
            corner_update.astype(jnp.bfloat16),
            preferred_element_type=jnp.float32,
        )
        image = assemble((apply_local + spread_corners) * live[:, :, None])
        curve = lax.psum(column_sums(direction, image), ("span", "sub"))
        alpha = norm_now / curve
        solution = solution + alpha * direction
        residual = residual - alpha * image
        norm_next = lax.psum(column_sums(residual, residual), ("span", "sub"))
        direction = residual + norm_next / norm_now * direction
        norm_now = norm_next
    return (solution, residual)


def solution(mesh):
    placed = (
        P(("span", "sub"), None, None),
        P(None, ("span", "sub"), None),
        P(),
        P(),
        P(("span", "sub"), None),
        P(("span", "sub")),
        P(("span", "sub"), None),
        P(("span", "sub"), None, None),
        P(("span", "sub"), None, None),
        P("span", None, None),
    )
    return jax.shard_map(
        on_device,
        mesh=mesh,
        in_specs=placed,
        out_specs=(P(("span", "sub"), None), P(("span", "sub"), None)),
        check_vma=False,
    )
```

profile of v0, /device:TPU:1, one launch (start us, length us, event | category | flops | bytes accessed | tf_op | source)
XLA Modules:
  0.0 475.8 jit_solution(13964561409451314039)
XLA Ops:
  0.6 0.0 copy-start
  1.4 1.3 multiply_reduce_fusion.5
  2.7 0.7 fusion.43
  3.4 0.8 multiply_reduce_fusion.4
  4.3 1.4 fusion.46
  5.6 6.9 %scatter_custom_fusion = f32[768,128]{1,0:T(8,128)S(1)} fusion(s32[768]{0:T(1024)S(1)} %fusion.43, bf16[1,768,128]{2,1,0:T(8,128)(2,1)} %param.10, f32[768]{0:T(1024)S(1)} %fusion.41, f32[768]{0:T(1024)S(1)} %multiply_reduce_fusion.4, f32[768]{0:T(1024)S(1)} %fusion.46, f32[]{:T(128)} %constant.45.clone.1), kind=kCustom, calls=%fused_computation.25 | custom fusion | flops 491520 | bytes 602116 | tf_op jit(solution)/shard_map/scatter-add | solution.py:63
  12.5 1.3 collective-permute-start
  13.8 4.6 collective-permute-start.1
  18.4 0.4 collective-permute-done
  18.8 1.5 collective-permute-done.1
  20.4 0.0 copy-start.1
  20.4 1.4 collective-permute-start.3
  21.8 4.4 collective-permute-start.2
  26.2 0.0 collective-permute-done.3
  26.3 1.8 collective-permute-done.2
  28.1 1.9 gather_fusion
  30.0 0.0 copy-done.1
  30.0 0.0 copy-start.2
  30.0 0.4 fusion.8
  30.4 50.9 %psum.43 = bf16[128,128]{0,1:T(8,128)(2,1)S(1)} all-reduce(bf16[128,128]{0,1:T(8,128)(2,1)S(1)} %fusion.8), channel_id=1, replica_groups=mesh['span'=32,'sub'=16] {'sub'}, use_global_device_ids=true, to_apply=%region_5.6 | all-reduce | flops 16384 | bytes 65536 | tf_op jit(solution)/shard_map/psum | solution.py:88
  81.3 0.0 copy-done
  81.3 0.6 fusion.6
  81.9 0.0 copy-done.2
  81.9 0.2 convolution_convert_fusion.1
  82.1 0.2 fusion.1
  82.3 0.2 copy.14
  82.5 6.1 %scatter_custom_fusion.1 = f32[768,128]{1,0:T(8,128)S(1)} fusion(s32[768]{0:T(1024)S(1)} %fusion.43, f32[768,128]{1,0:T(8,128)S(1)} %copy.14, f32[]{:T(128)} %constant.45.clone.1), kind=kCustom, calls=%fused_computation.44 | custom fusion | flops 98304 | bytes 393220 | tf_op jit(solution)/shard_map/scatter-add | solution.py:63
  88.7 1.3 collective-permute-start.4
  90.0 4.6 collective-permute-start.5
  94.6 0.4 collective-permute-done.4
  95.0 1.5 collective-permute-done.5
  96.5 0.1 multiply_reduce_fusion.2
  96.6 109.2 %all-reduce = (f32[128]{0:T(128)S(1)}, f32[128]{0:T(128)S(1)}) all-reduce(f32[128]{0:T(128)S(1)} %get-tuple-element.3, f32[128]{0:T(128)S(1)} %get-tuple-element.2), channel_id=1, replica_groups=mesh['span'=32,'sub'=16] {'span','sub'}, use_global_device_ids=true, to_apply=%region_4.5 | all-reduce | flops 256 | bytes 2048 | tf_op jit(solution)/shard_map/psum | solution.py:74
  205.7 0.1 multiply_reduce_fusion.1
  205.8 95.3 %psum.45 = f32[128]{0:T(128)S(1)} all-reduce(f32[128]{0:T(128)S(1)} %multiply_reduce_fusion.1), channel_id=1, replica_groups=mesh['span'=32,'sub'=16] {'span','sub'}, use_global_device_ids=true, to_apply=%region_10.11 | all-reduce | flops 128 | bytes 1024 | tf_op jit(solution)/shard_map/psum | solution.py:101
  301.1 1.3 collective-permute-start.7
  302.4 4.0 collective-permute-start.6
  306.4 0.0 collective-permute-done.7
  306.4 1.3 collective-permute-done.6
  307.7 1.9 gather_fusion.1
  309.6 0.4 fusion.9
  310.0 0.6 fusion.4
  310.6 44.2 %psum.46 = bf16[128,128]{0,1:T(8,128)(2,1)S(1)} all-reduce(bf16[128,128]{0,1:T(8,128)(2,1)S(1)} %fusion.9), channel_id=1, replica_groups=mesh['span'=32,'sub'=16] {'sub'}, use_global_device_ids=true, to_apply=%region_11.12 | all-reduce | flops 16384 | bytes 65536 | tf_op jit(solution)/shard_map/psum | solution.py:88
  354.8 0.2 convolution_convert_fusion
  355.0 0.2 fusion.3
  355.3 0.2 copy.15
  355.4 6.1 %scatter_custom_fusion.2 = f32[768,128]{1,0:T(8,128)S(1)} fusion(s32[768]{0:T(1024)S(1)} %fusion.43, f32[768,128]{1,0:T(8,128)S(1)} %copy.15, f32[]{:T(128)} %constant.45.clone.1), kind=kCustom, calls=%fused_computation.42 | custom fusion | flops 98304 | bytes 393220 | tf_op jit(solution)/shard_map/scatter-add | solution.py:63
  361.6 1.3 collective-permute-start.8
  362.9 4.6 collective-permute-start.9
  367.5 0.4 collective-permute-done.8
  367.9 1.5 collective-permute-done.9
  369.5 0.1 multiply_reduce_fusion
  369.5 105.5 %psum.47 = f32[128]{0:T(128)S(1)} all-reduce(f32[128]{0:T(128)S(1)} %multiply_reduce_fusion), channel_id=1, replica_groups=mesh['span'=32,'sub'=16] {'span','sub'}, use_global_device_ids=true, to_apply=%region_14.15 | all-reduce | flops 128 | bytes 1024 | tf_op jit(solution)/shard_map/psum | solution.py:97
  475.0 0.8 multiply_subtract_fusion
  (12 shorter events, 0.2 us)
Async XLA Ops:
  0.6 80.6 %copy-start = (bf16[1,768,768]{2,1,0:T(8,128)(2,1)S(1)}, bf16[1,768,768]{2,1,0:T(8,128)(2,1)}, u32[]{:S(2)}) copy-start(bf16[1,768,768]{2,1,0:T(8,128)(2,1)} %param.17) | copy-start | bytes 3538948
  12.5 6.3 %collective-permute-start = (f32[256,128]{1,0:T(8,128)S(1)}, f32[256,128]{1,0:T(8,128)S(1)}, u32[]{:S(2)}, u32[]{:S(2)}) collective-permute-start(f32[256,128]{1,0:T(8,128)S(1)} %get-tuple-element.15), channel_id=1, source_target_pairs={{16,0},{32,16},{48,32},{64,48},{80,64},{96,80},{112,96},{128,112},... | collective-permute-start | bytes 393224 | tf_op jit(solution)/shard_map/ppermute | solution.py:12
  13.8 6.5 %collective-permute-start.1 = (f32[256,128]{1,0:T(8,128)S(1)}, f32[256,128]{1,0:T(8,128)S(1)}, u32[]{:S(2)}, u32[]{:S(2)}) collective-permute-start(f32[256,128]{1,0:T(8,128)S(1)} %get-tuple-element.16), channel_id=1, source_target_pairs={{0,16},{16,32},{32,48},{48,64},{64,80},{80,96},{96,112},{112,128},... | collective-permute-start | bytes 393224 | tf_op jit(solution)/shard_map/ppermute | solution.py:12
  20.4 9.6 %copy-start.1 = (bf16[1,768,128]{2,1,0:T(8,128)(2,1)S(1)}, bf16[1,768,128]{2,1,0:T(8,128)(2,1)}, u32[]{:S(2)}) copy-start(bf16[1,768,128]{2,1,0:T(8,128)(2,1)} %param.18) | copy-start | bytes 589828
  20.4 5.9 %collective-permute-start.3 = (bf16[256,128]{1,0:T(8,128)(2,1)S(1)}, bf16[256,128]{1,0:T(8,128)(2,1)S(1)}, u32[]{:S(2)}, u32[]{:S(2)}) collective-permute-start(bf16[256,128]{1,0:T(8,128)(2,1)S(1)} %get-tuple-element.7), channel_id=1, source_target_pairs={{16,0},{32,16},{48,32},{64,48},{80,64},{96,80},{112,96},{128,112},... | collective-permute-start | bytes 196616 | tf_op jit(solution)/shard_map/ppermute | solution.py:23
  21.8 6.3 %collective-permute-start.2 = (bf16[256,128]{1,0:T(8,128)(2,1)S(1)}, bf16[256,128]{1,0:T(8,128)(2,1)S(1)}, u32[]{:S(2)}, u32[]{:S(2)}) collective-permute-start(bf16[256,128]{1,0:T(8,128)(2,1)S(1)} %get-tuple-element.7), channel_id=1, source_target_pairs={{0,16},{16,32},{32,48},{48,64},{64,80},{80,96},{96,112},{112,128},... | collective-permute-start | bytes 196616 | tf_op jit(solution)/shard_map/ppermute | solution.py:22
  30.0 51.9 %copy-start.2 = (f32[1,128,128]{2,1,0:T(8,128)S(1)}, f32[1,128,128]{2,1,0:T(8,128)}, u32[]{:S(2)}) copy-start(f32[1,128,128]{2,1,0:T(8,128)} %param.19) | copy-start | bytes 196612
  88.7 6.3 %collective-permute-start.4 = (f32[256,128]{1,0:T(8,128)S(1)}, f32[256,128]{1,0:T(8,128)S(1)}, u32[]{:S(2)}, u32[]{:S(2)}) collective-permute-start(f32[256,128]{1,0:T(8,128)S(1)} %get-tuple-element.13), channel_id=1, source_target_pairs={{16,0},{32,16},{48,32},{64,48},{80,64},{96,80},{112,96},{128,112},... | collective-permute-start | bytes 393224 | tf_op jit(solution)/shard_map/ppermute | solution.py:12
  90.0 6.5 %collective-permute-start.5 = (f32[256,128]{1,0:T(8,128)S(1)}, f32[256,128]{1,0:T(8,128)S(1)}, u32[]{:S(2)}, u32[]{:S(2)}) collective-permute-start(f32[256,128]{1,0:T(8,128)S(1)} %get-tuple-element.14), channel_id=1, source_target_pairs={{0,16},{16,32},{32,48},{48,64},{64,80},{80,96},{96,112},{112,128},... | collective-permute-start | bytes 393224 | tf_op jit(solution)/shard_map/ppermute | solution.py:12
  301.1 5.3 %collective-permute-start.7 = (bf16[256,128]{1,0:T(8,128)(2,1)S(1)}, bf16[256,128]{1,0:T(8,128)(2,1)S(1)}, u32[]{:S(2)}, u32[]{:S(2)}) collective-permute-start(bf16[256,128]{1,0:T(8,128)(2,1)S(1)} %fusion.47), channel_id=1, source_target_pairs={{16,0},{32,16},{48,32},{64,48},{80,64},{96,80},{112,96},{128,112},... | collective-permute-start | bytes 196616 | tf_op jit(solution)/shard_map/ppermute | solution.py:23
  302.4 5.3 %collective-permute-start.6 = (bf16[256,128]{1,0:T(8,128)(2,1)S(1)}, bf16[256,128]{1,0:T(8,128)(2,1)S(1)}, u32[]{:S(2)}, u32[]{:S(2)}) collective-permute-start(bf16[256,128]{1,0:T(8,128)(2,1)S(1)} %fusion.47), channel_id=1, source_target_pairs={{0,16},{16,32},{32,48},{48,64},{64,80},{80,96},{96,112},{112,128},... | collective-permute-start | bytes 196616 | tf_op jit(solution)/shard_map/ppermute | solution.py:22
  361.6 6.3 %collective-permute-start.8 = (f32[256,128]{1,0:T(8,128)S(1)}, f32[256,128]{1,0:T(8,128)S(1)}, u32[]{:S(2)}, u32[]{:S(2)}) collective-permute-start(f32[256,128]{1,0:T(8,128)S(1)} %get-tuple-element.11), channel_id=1, source_target_pairs={{16,0},{32,16},{48,32},{64,48},{80,64},{96,80},{112,96},{128,112},... | collective-permute-start | bytes 393224 | tf_op jit(solution)/shard_map/ppermute | solution.py:12
  362.9 6.6 %collective-permute-start.9 = (f32[256,128]{1,0:T(8,128)S(1)}, f32[256,128]{1,0:T(8,128)S(1)}, u32[]{:S(2)}, u32[]{:S(2)}) collective-permute-start(f32[256,128]{1,0:T(8,128)S(1)} %get-tuple-element.12), channel_id=1, source_target_pairs={{0,16},{16,32},{32,48},{48,64},{64,80},{80,96},{96,112},{112,128},... | collective-permute-start | bytes 393224 | tf_op jit(solution)/shard_map/ppermute | solution.py:12
where the time goes:
time: 477 us; the launch traced here: 476 us
  blocking collectives  405 us (85%)
  starting transfers between devices  28.8 us (6%)
  other arithmetic  24.3 us (5%)
  waiting for transfers between devices  8.91 us (2%)
    psum x1, blocking collectives, on_device(): norm_now = lax.psum(column_sums(residual, residual), ('span', 'sub'))  109 us
    psum x1, blocking collectives, on_device(): curve = lax.psum(column_sums(direction, image), ('span', 'sub'))  106 us
    psum x1, blocking collectives, on_device(): norm_next = lax.psum(column_sums(residual, residual), ('span', 'sub'))  95.3 us
    psum x2, blocking collectives, on_device(): lax.psum(corner_part.astype(jnp.bfloat16), 'sub').astype(jnp.float32)  95.1 us
    scatter-add x3, other arithmetic, assemble(): jnp.zeros((3 * owned, loads), jnp.float32).at[window_pos]  19.1 us
    ppermute x6, starting transfers between devices, from_behind(): return lax.ppermute(shard, axis, pairs)  17.7 us
  transfers between devices with their start and end apart: 10, of which 8 were waited for; matrix products, arithmetic and copies ran while one was open for 0% of the time, Pallas kernels for 0%

commit v1 on v0

v1 whole, which is shorter than its diff:
```python
import functools

import jax
import jax.numpy as jnp
from jax import lax
from jax.experimental import pallas as pl
from jax.experimental.pallas import tpu as pltpu
from jax.sharding import PartitionSpec as P

MESH = pl.DeviceIdType.MESH
F32 = jnp.float32
BF16 = jnp.bfloat16
CONTRIB = jnp.bfloat16
OWN = 256
SLOTS = 768
CASES = 128
CORNERS = 128
HALF = CORNERS // 2
SUMS = 16
ROWS = 64


def dot(a, b):
    return jnp.dot(a, b, preferred_element_type=F32)


def two_parts(x):
    high = x.astype(BF16)
    return high, (x - high.astype(F32)).astype(BF16)


def column_sum(x):
    return jnp.sum(x, axis=0, keepdims=True)


def as_column(row):
    return jnp.transpose(jnp.broadcast_to(row, (CASES, SLOTS)))


def sum_rows(first, second):
    row = lax.broadcasted_iota(jnp.int32, (SUMS, CASES), 0)
    out = jnp.zeros((SUMS, CASES), F32)
    for base, value in ((0, first), (3, second)):
        rest = value
        for i in range(3):
            part = rest.astype(BF16).astype(F32)
            rest = rest - part
            out = jnp.where(row == base + i, part, out)
    return out


def kernel(
    spans,
    subs,
    retard,
    compliance,
    lengths,
    stress_hbm,
    history_hbm,
    micro_hbm,
    index_hbm,
    dual_hbm,
    corner_hbm,
    stiff_hbm,
    solution_ref,
    residual_ref,
    stress,
    history,
    micro,
    index,
    dual,
    corner,
    stiff,
    pick,
    pick_t,
    corner_t,
    corner_w,
    split,
    window,
    local_window,
    v,
    contrib_out,
    contrib_in,
    w_part,
    w_full,
    chip_in,
    ring_out,
    ring_in,
    pair_out,
    pair_in,
    totals,
    load_sem,
    contrib_send,
    contrib_recv,
    halo_send,
    halo_recv,
    chip_sem,
    ring_send,
    ring_recv,
    pair_sem,
    total_send,
    total_recv,
):
    p = lax.axis_index("span")
    s = lax.axis_index("sub")
    chips = subs // 2
    core = lax.rem(s, 2)
    partner = (p, s + 1 - 2 * core)
    before = (lax.rem(p + spans - 1, spans), s)
    after = (lax.rem(p + 1, spans), s)
    mine = pl.ds(pl.multiple_of(core * HALF, HALF), HALF)
    theirs = pl.ds(pl.multiple_of((1 - core) * HALF, HALF), HALF)

    loads = [
        pltpu.make_async_copy(src, dst, load_sem.at[i])
        for i, (src, dst) in enumerate(
            (
                (index_hbm, index),
                (micro_hbm, micro),
                (history_hbm, history),
                (stress_hbm.at[0], stress),
                (corner_hbm.at[0], corner),
                (dual_hbm.at[0], dual),
                (stiff_hbm.at[0], stiff),
            )
        )
    ]
    for copy in loads:
        copy.start()

    barrier = pltpu.get_barrier_semaphore()

    def greet_span(d, carry):
        pl.semaphore_signal(
            barrier, inc=1, device_id=(lax.rem(p + d, spans), s), device_id_type=MESH
        )
        return carry

    def greet_chip(d, carry):
        pl.semaphore_signal(
            barrier, inc=1, device_id=(p, lax.rem(s + 2 * d, subs)), device_id_type=MESH
        )
        return carry

    lax.fori_loop(1, spans, greet_span, 0)
    lax.fori_loop(1, chips, greet_chip, 0)
    pl.semaphore_signal(barrier, inc=1, device_id=partner, device_id_type=MESH)

    loads[0].wait()
    slot = lax.broadcasted_iota(jnp.int32, (1, SLOTS), 1)
    owner_span = index[...] // (OWN * subs)
    place = (owner_span - p + 1) * OWN + lax.rem(index[...], OWN)
    place = jnp.where(slot < lengths[0], place, -1)

    def build_pick(i, carry):
        rows = pl.ds(pl.multiple_of(i * ROWS, ROWS), ROWS)
        at = lax.broadcasted_iota(jnp.int32, (ROWS, SLOTS), 0) + i * ROWS
        pick[rows, :] = jnp.where(at == place, 1.0, 0.0).astype(BF16)
        return carry

    lax.fori_loop(0, SLOTS // ROWS, build_pick, 0)

    loads[1].wait()
    loads[2].wait()
    creep = jnp.zeros((1, SLOTS), F32)
    past = jnp.zeros((1, SLOTS), F32)
    for k in range(history.shape[0]):
        weight = 1.0 - jnp.exp(-1.0 / jnp.full((1, SLOTS), retard[k], F32))
        creep = creep + weight * compliance[k]
        past = past + weight * history[k]
    relaxed = micro[...] / (1.0 + micro[...])
    scale = as_column(creep + 0.5 * relaxed)
    past = as_column(past)
    loads[3].wait()
    load = scale * stress[...].astype(F32) - past
    high, low = two_parts(load)
    split[:, :CASES] = high
    split[:, CASES:] = low

    def picked(rows):
        both = dot(pick[rows, :], split[...])
        return both[:, :CASES] + both[:, CASES:]

    def contrib_copies(k):
        return [
            pltpu.make_async_remote_copy(
                src_ref=contrib_out.at[k, i],
                dst_ref=contrib_in.at[k, i],
                send_sem=contrib_send.at[k, i],
                recv_sem=contrib_recv.at[k, i],
                device_id=to,
                device_id_type=MESH,
            )
            for i, to in enumerate((before, after))
        ]

    def halo_copies(k):
        return [
            pltpu.make_async_remote_copy(
                src_ref=window.at[k, pl.ds(OWN, OWN)],
                dst_ref=window.at[k, pl.ds(2 * OWN if i == 0 else 0, OWN)],
                send_sem=halo_send.at[k, i],
                recv_sem=halo_recv.at[k, i],
                device_id=to,
                device_id_type=MESH,
            )
            for i, to in enumerate((before, after))
        ]

    def chip_copy(k):
        return pltpu.make_async_remote_copy(
            src_ref=w_part.at[k, theirs],
            dst_ref=chip_in.at[k],
            send_sem=chip_sem.at[k, 0],
            recv_sem=chip_sem.at[k, 1],
            device_id=partner,
            device_id_type=MESH,
        )

    def ring_copies(k):
        return [
            pltpu.make_async_remote_copy(
                src_ref=ring_out.at[k],
                dst_ref=ring_in.at[k, d - 1],
                send_sem=ring_send.at[k, d - 1],
                recv_sem=ring_recv.at[k, d - 1],
                device_id=(p, lax.rem(s + 2 * d, subs)),
                device_id_type=MESH,
            )
            for d in range(1, chips)
        ]

    def pair_copy(k):
        return pltpu.make_async_remote_copy(
            src_ref=pair_out.at[k],
            dst_ref=pair_in.at[k],
            send_sem=pair_sem.at[k, 0],
            recv_sem=pair_sem.at[k, 1],
            device_id=partner,
            device_id_type=MESH,
        )

    def total_copy(k, d):
        return pltpu.make_async_remote_copy(
            src_ref=totals.at[k, 0],
            dst_ref=totals.at[k, d],
            send_sem=total_send.at[k, d],
            recv_sem=total_recv.at[k, d],
            device_id=(lax.rem(p + d, spans), s),
            device_id_type=MESH,
        )

    def each_total(k, act):
        def step(d, carry):
            act(total_copy(k, d))
            return carry

        lax.fori_loop(1, spans, step, 0)

    previous, own, following = (slice(i * OWN, (i + 1) * OWN) for i in range(3))

    def assembled(k, own_part):
        for copy in contrib_copies(k):
            copy.wait_recv()
        return own_part + contrib_in[k, 0].astype(F32) + contrib_in[k, 1].astype(F32)

    contrib_out[0, 0] = picked(previous).astype(CONTRIB)
    contrib_out[0, 1] = picked(following).astype(CONTRIB)
    pl.semaphore_wait(barrier, spans + chips - 1)
    for copy in contrib_copies(0):
        copy.start()
    own_part = picked(own)

    place_t = as_column(place.astype(F32))

    def build_pick_t(j, carry):
        lanes = pl.ds(pl.multiple_of(j * CASES, CASES), CASES)
        at = lax.broadcasted_iota(jnp.int32, (SLOTS, CASES), 1) + j * CASES
        pick_t[:, lanes] = jnp.where(place_t == at.astype(F32), 1.0, 0.0).astype(BF16)
        return carry

    lax.fori_loop(0, SLOTS // CASES, build_pick_t, 0)
    loads[4].wait()
    corner_t[...] = jnp.transpose(corner[...].astype(F32)).astype(BF16)
    high, low = two_parts(dot(pick[...], corner[...]))
    corner_w[:, :CORNERS] = high
    corner_w[:, CORNERS:] = low
    loads[5].wait()
    loads[6].wait()

    v[0] = assembled(0, own_part)
    for k in range(2):
        window[k, own] = v[k].astype(BF16)
        for copy in halo_copies(k):
            copy.start()
        norm = column_sum(v[k] * v[k])
        for copy in halo_copies(k):
            copy.wait_recv()
        u = dot(pick_t[...], window[k]).astype(BF16)
        w_part[k] = dot(corner_t[...], u)
        chip_copy(k).start()
        y = dot(dual[...], u)
        ring_sums = sum_rows(norm, column_sum(u.astype(F32) * y))
        chip_copy(k).wait_recv()
        half = w_part[k, mine] + chip_in[k]
        ring_out[k, :HALF] = half.astype(BF16)
        ring_out[k, HALF:] = ring_sums.astype(BF16)
        for copy in ring_copies(k):
            copy.start()
        high, low = two_parts(y)
        split[:, :CASES] = high
        split[:, CASES:] = low
        for block in (previous, own, following):
            local_window[block, :] = picked(block)
        for d, copy in enumerate(ring_copies(k)):
            copy.wait_recv()
        for d in range(chips - 1):
            half = half + ring_in[k, d, :HALF].astype(F32)
            ring_sums = ring_sums + ring_in[k, d, HALF:].astype(F32)
        pair_out[k, :HALF] = half
        pair_out[k, HALF:] = ring_sums
        pair_copy(k).start()
        w_full[mine, :] = half
        pair_copy(k).wait_recv()
        w_full[theirs, :] = pair_in[k, :HALF]
        ring_sums = ring_sums + pair_in[k, HALF:]
        w = w_full[...]
        z = jnp.dot(stiff[...], w, precision=lax.Precision.HIGHEST, preferred_element_type=F32)
        z_narrow = z.astype(BF16)
        z_twice = jnp.concatenate([z_narrow, z_narrow], axis=0)

        def image(rows):
            return local_window[rows, :] + dot(corner_w[rows, :], z_twice)

        contrib_out[k + 1, 0] = image(previous).astype(CONTRIB)
        contrib_out[k + 1, 1] = image(following).astype(CONTRIB)
        for copy in contrib_copies(k + 1):
            copy.start()
        coarse = column_sum(w * z_narrow.astype(F32))
        totals[k, 0] = jnp.concatenate(
            [column_sum(ring_sums[0:3]), column_sum(ring_sums[3:6]) + coarse], axis=0
        )
        each_total(k, lambda copy: copy.start())
        own_part = image(own)
        v[k + 1] = assembled(k + 1, own_part)

    for k in range(2):
        each_total(k, lambda copy: copy.wait_recv())
    first = jnp.sum(totals[0], axis=0)
    second = jnp.sum(totals[1], axis=0)
    g00, g01 = first[0:1], first[1:2]
    g11, g12 = second[0:1], second[1:2]
    alpha0 = g00 / g01
    norm1 = g00 - 2.0 * alpha0 * g01 + alpha0 * alpha0 * g11
    beta = norm1 / g00
    grown = 1.0 + beta
    curve = grown * grown * g01 - 2.0 * grown * alpha0 * g11 + alpha0 * alpha0 * g12
    alpha1 = norm1 / curve
    v0, v1, v2 = v[0], v[1], v[2]
    residual1 = v0 - alpha0 * v1
    direction1 = residual1 + beta * v0
    solution_ref[...] = alpha0 * v0 + alpha1 * direction1
    residual_ref[...] = residual1 - alpha1 * (grown * v1 - alpha0 * v2)

    for k in range(3):
        for copy in contrib_copies(k):
            copy.wait_send()
    for k in range(2):
        for copy in halo_copies(k) + [chip_copy(k), pair_copy(k)] + ring_copies(k):
            copy.wait_send()
        each_total(k, lambda copy: copy.wait_send())


def solution(mesh):
    spans, subs = mesh.shape["span"], mesh.shape["sub"]
    chips = subs // 2
    vmem = pl.BlockSpec(memory_space=pltpu.VMEM)
    smem = pl.BlockSpec(memory_space=pltpu.SMEM)
    hbm = pl.BlockSpec(memory_space=pl.ANY)
    dma = pltpu.SemaphoreType.DMA

    def on_device(
        stress,
        history,
        retard,
        compliance,
        micro,
        lengths,
        multiplier_index,
        dual_block,
        corner_map,
        coarse_stiffness_inverse,
    ):
        units = history.shape[0]
        return pl.pallas_call(
            functools.partial(kernel, spans, subs),
            name="creep_step",
            out_shape=[jax.ShapeDtypeStruct((OWN, CASES), F32)] * 2,
            in_specs=[smem] * 3 + [hbm] * 7,
            out_specs=[vmem] * 2,
            scratch_shapes=[
                pltpu.VMEM((SLOTS, CASES), BF16),
                pltpu.VMEM((units, 1, SLOTS), F32),
                pltpu.VMEM((1, SLOTS), F32),
                pltpu.VMEM((1, SLOTS), jnp.int32),
                pltpu.VMEM((SLOTS, SLOTS), BF16),
                pltpu.VMEM((SLOTS, CORNERS), BF16),
                pltpu.VMEM((CORNERS, CORNERS), F32),
                pltpu.VMEM((SLOTS, SLOTS), BF16),
                pltpu.VMEM((SLOTS, SLOTS), BF16),
                pltpu.VMEM((CORNERS, SLOTS), BF16),
                pltpu.VMEM((SLOTS, 2 * CORNERS), BF16),
                pltpu.VMEM((SLOTS, 2 * CASES), BF16),
                pltpu.VMEM((2, SLOTS, CASES), BF16),
                pltpu.VMEM((SLOTS, CASES), F32),
                pltpu.VMEM((3, OWN, CASES), F32),
                pltpu.VMEM((3, 2, OWN, CASES), CONTRIB),
                pltpu.VMEM((3, 2, OWN, CASES), CONTRIB),
                pltpu.VMEM((2, CORNERS, CASES), F32),
                pltpu.VMEM((CORNERS, CASES), F32),
                pltpu.VMEM((2, HALF, CASES), F32),
                pltpu.VMEM((2, HALF + SUMS, CASES), BF16),
                pltpu.VMEM((2, chips - 1, HALF + SUMS, CASES), BF16),
                pltpu.VMEM((2, HALF + SUMS, CASES), F32),
                pltpu.VMEM((2, HALF + SUMS, CASES), F32),
                pltpu.VMEM((2, spans, 2, CASES), F32),
                dma((7,)),
                dma((3, 2)),
                dma((3, 2)),
                dma((2, 2)),
                dma((2, 2)),
                dma((2, 2)),
                dma((2, chips - 1)),
                dma((2, chips - 1)),
                dma((2, 2)),
                dma((2, spans)),
                dma((2, spans)),
            ],
            compiler_params=pltpu.CompilerParams(
                collective_id=0, has_side_effects=True, vmem_limit_bytes=32 * 2**20
            ),
        )(
            retard,
            compliance,
            lengths,
            stress,
            history,
            micro,
            multiplier_index,
            dual_block,
            corner_map,
            coarse_stiffness_inverse,
        )

    rows = P(("span", "sub"), None)
    blocks = P(("span", "sub"), None, None)
    return jax.shard_map(
        on_device,
        mesh=mesh,
        in_specs=(
            blocks,
            P(None, ("span", "sub"), None),
            P(),
            P(),
            rows,
            P(("span", "sub")),
            rows,
            blocks,
            blocks,
            P("span", None, None),
        ),
        out_specs=(rows, rows),
        check_vma=False,
    )
```

time: 477 us -> 76.5 us (0.16)
  blocking collectives: 405 us -> 0 us
  Pallas kernels: 0 us -> 66.1 us
  starting transfers between devices: 28.8 us -> 0 us
  other arithmetic: 24.3 us -> 0 us
  waiting for transfers between devices: 8.91 us -> 0 us
    psum x5 -> x0, blocking collectives: 405 us -> none  [the longest x1 109 us: on_device(): norm_now = lax.psum(column_sums(residual, residual), ('span', 'sub'))]
    pallas_call x0 -> x1, Pallas kernels: none -> 66.1 us  [on_device(): pl.pallas_call(functools.partial(kernel, spans, subs), name='creep_step',...]
    ppermute x10 -> x0, starting transfers between devices: 28.8 us -> none  [the longest x6 17.7 us: from_behind(): return lax.ppermute(shard, axis, pairs)]
    scatter-add x3 -> x0, other arithmetic: 19.1 us -> none  [assemble(): jnp.zeros((3 * owned, loads), jnp.float32).at[window_pos]]
    ppermute x10 -> x0, waiting for transfers between devices: 8.91 us -> none  [the longest x6 5.77 us: from_behind(): return lax.ppermute(shard, axis, pairs)]
    unnamed x6 -> x20, local copies, waits for them, and re-layouts: 0.02 us -> 8.68 us
  transfers between devices with their start and end apart: 10 -> 0, of which waited for: 8 -> 0; matrix products, arithmetic and copies ran while one was open for 0% -> 0% of each run, Pallas kernels for 0% -> 0%
where the time goes in v1:
time: 76.5 us; the launch traced here: 76.1 us
  Pallas kernels  66.1 us (86%)
  local copies, waits for them, and re-layouts  8.68 us (11%)
  between operations  1.3 us (2%)
    pallas_call x1, Pallas kernels, on_device(): pl.pallas_call(functools.partial(kernel, spans, subs), name='creep_step',...  66.1 us
    unnamed x20, local copies, waits for them, and re-layouts  8.68 us

profile of v1, /device:TPU:1, one launch (start us, length us, event | category | flops | bytes accessed | tf_op | source)
XLA Modules:
  0.0 76.1 jit_solution(17704630213659287725)
XLA Ops:
  1.3 0.0 copy-start
  1.3 1.3 %copy-done = bf16[1,768,768]{2,1,0:T(8,128)(2,1)S(1)} copy-done((bf16[1,768,768]{2,1,0:T(8,128)(2,1)S(1)}, bf16[1,768,768]{2,1,0:T(8,128)(2,1)}, u32[]{:S(2)}) %copy-start) | copy-done | bytes 1179672
  2.6 0.0 copy-start.1
  2.6 0.9 %copy-done.1 = bf16[1,768,128]{2,1,0:T(8,128)(2,1)S(1)} copy-done((bf16[1,768,128]{2,1,0:T(8,128)(2,1)S(1)}, bf16[1,768,128]{2,1,0:T(8,128)(2,1)}, u32[]{:S(2)}) %copy-start.1) | copy-done | bytes 196632
  3.5 0.0 copy-start.2
  3.5 0.9 %copy-done.2 = bf16[1,768,128]{2,1,0:T(8,128)(2,1)S(1)} copy-done((bf16[1,768,128]{2,1,0:T(8,128)(2,1)S(1)}, bf16[1,768,128]{2,1,0:T(8,128)(2,1)}, u32[]{:S(2)}) %copy-start.2) | copy-done | bytes 196632
  4.4 0.0 copy-start.3
  4.4 0.8 %copy-done.3 = f32[1,128,128]{2,1,0:T(8,128)S(1)} copy-done((f32[1,128,128]{2,1,0:T(8,128)S(1)}, f32[1,128,128]{2,1,0:T(8,128)}, u32[]{:S(2)}) %copy-start.3) | copy-done | bytes 65560
  5.2 0.0 copy-start.4
  5.2 0.7 copy-done.4
  6.0 0.0 copy-start.5
  6.0 0.7 copy-done.5
  6.7 0.0 copy-start.6
  6.7 0.7 copy-done.6
  7.4 0.0 copy-start.7
  7.4 0.7 copy-done.7
  8.0 0.0 copy-start.8
  8.0 0.7 copy-done.8
  8.7 66.1 %creep_step.1 = (f32[256,128]{1,0:T(8,128)S(1)}, f32[256,128]{1,0:T(8,128)S(1)}) custom-call(f32[8]{0:T(128)S(1)} %copy-done.7, f32[8]{0:T(128)S(1)} %copy-done.8, s32[1]{0:T(128)S(6)} %copy.14.lengths, bf16[1,768,128]{2,1,0:T(8,128)(2,1)S(1)} %copy-done.1, f32[8,1,768]{2,1,0:T(1,128)S(1)} %copy-done.4, f32[1,768]{1,0:T(1,128)S(1)} %copy-done.5, ...), custom_call_target="tpu_custom_call" | custom-call | tf_op jit(solution)/shard_map/creep_step/pallas_call | solution.py:395
  74.7 0.7 copy.15
  75.4 0.7 copy.16
Async XLA Ops:
  1.3 1.3 %copy-start = (bf16[1,768,768]{2,1,0:T(8,128)(2,1)S(1)}, bf16[1,768,768]{2,1,0:T(8,128)(2,1)}, u32[]{:S(2)}) copy-start(bf16[1,768,768]{2,1,0:T(8,128)(2,1)} %dual_hbm.1) | copy-start | bytes 3538948
  2.6 0.9 %copy-start.1 = (bf16[1,768,128]{2,1,0:T(8,128)(2,1)S(1)}, bf16[1,768,128]{2,1,0:T(8,128)(2,1)}, u32[]{:S(2)}) copy-start(bf16[1,768,128]{2,1,0:T(8,128)(2,1)} %stress_hbm.1) | copy-start | bytes 589828
  3.5 0.9 %copy-start.2 = (bf16[1,768,128]{2,1,0:T(8,128)(2,1)S(1)}, bf16[1,768,128]{2,1,0:T(8,128)(2,1)}, u32[]{:S(2)}) copy-start(bf16[1,768,128]{2,1,0:T(8,128)(2,1)} %corner_hbm.1) | copy-start | bytes 589828
  4.4 0.8 %copy-start.3 = (f32[1,128,128]{2,1,0:T(8,128)S(1)}, f32[1,128,128]{2,1,0:T(8,128)}, u32[]{:S(2)}) copy-start(f32[1,128,128]{2,1,0:T(8,128)} %stiff_hbm.1) | copy-start | bytes 196612
  5.2 0.7 copy-start.4
  6.0 0.7 copy-start.5
  6.7 0.7 copy-start.6
  7.4 0.7 copy-start.7
  8.0 0.7 copy-start.8

commit v2 on v1

--- a/solution.py
+++ b/solution.py
@@ -92,8 +92,6 @@
     load_sem,
     contrib_send,
     contrib_recv,
-    halo_send,
-    halo_recv,
     chip_sem,
     ring_send,
     ring_recv,
@@ -106,8 +104,6 @@
     chips = subs // 2
     core = lax.rem(s, 2)
     partner = (p, s + 1 - 2 * core)
-    before = (lax.rem(p + spans - 1, spans), s)
-    after = (lax.rem(p + 1, spans), s)
     mine = pl.ds(pl.multiple_of(core * HALF, HALF), HALF)
     theirs = pl.ds(pl.multiple_of((1 - core) * HALF, HALF), HALF)
 
@@ -181,31 +177,21 @@
         both = dot(pick[rows, :], split[...])
         return both[:, :CASES] + both[:, CASES:]
 
-    def contrib_copies(k):
-        return [
-            pltpu.make_async_remote_copy(
-                src_ref=contrib_out.at[k, i],
-                dst_ref=contrib_in.at[k, i],
-                send_sem=contrib_send.at[k, i],
-                recv_sem=contrib_recv.at[k, i],
-                device_id=to,
-                device_id_type=MESH,
-            )
-            for i, to in enumerate((before, after))
-        ]
-
-    def halo_copies(k):
-        return [
-            pltpu.make_async_remote_copy(
-                src_ref=window.at[k, pl.ds(OWN, OWN)],
-                dst_ref=window.at[k, pl.ds(2 * OWN if i == 0 else 0, OWN)],
-                send_sem=halo_send.at[k, i],
-                recv_sem=halo_recv.at[k, i],
-                device_id=to,
-                device_id_type=MESH,
-            )
-            for i, to in enumerate((before, after))
-        ]
+    routes = ((1, 1), (2, 2), (2, 1), (0, -1), (1, -1), (0, -2))
+
+    def contrib_copy(k, i):
+        block, onward = routes[i]
+        return pltpu.make_async_remote_copy(
+            src_ref=contrib_out.at[k, block],
+            dst_ref=contrib_in.at[k, i],
+            send_sem=contrib_send.at[k, i],
+            recv_sem=contrib_recv.at[k, i],
+            device_id=(lax.rem(p + spans + onward, spans), s),
+            device_id_type=MESH,
+        )
+
+    def used_routes(k):
+        return range(6) if k < 2 else (2, 3)
 
     def chip_copy(k):
         return pltpu.make_async_remote_copy(
@@ -257,19 +243,38 @@
 
         lax.fori_loop(1, spans, step, 0)
 
-    previous, own, following = (slice(i * OWN, (i + 1) * OWN) for i in range(3))
-
-    def assembled(k, own_part):
-        for copy in contrib_copies(k):
-            copy.wait_recv()
-        return own_part + contrib_in[k, 0].astype(F32) + contrib_in[k, 1].astype(F32)
-
-    contrib_out[0, 0] = picked(previous).astype(CONTRIB)
-    contrib_out[0, 1] = picked(following).astype(CONTRIB)
-    pl.semaphore_wait(barrier, spans + chips - 1)
-    for copy in contrib_copies(0):
-        copy.start()
-    own_part = picked(own)
+    previous, own, following = blocks = [slice(i * OWN, (i + 1) * OWN) for i in range(3)]
+
+    def send_contribs(k, image):
+        for block in (0, 2, 1) if k < 2 else (0, 2):
+            value = image(blocks[block])
+            if k < 2:
+                local_window[blocks[block], :] = value
+            contrib_out[k, block] = value.astype(CONTRIB)
+            if k == 0 and block == 0:
+                pl.semaphore_wait(barrier, spans + chips - 1)
+            for i in reversed(used_routes(k)):
+                if routes[i][0] == block:
+                    contrib_copy(k, i).start()
+        if k == 2:
+            local_window[own, :] = image(own)
+
+    def receive_contribs(k):
+        for i in used_routes(k):
+            contrib_copy(k, i).wait_recv()
+
+        def arrived(i):
+            return contrib_in[k, i].astype(F32)
+
+        v[k] = local_window[own, :] + arrived(2) + arrived(3)
+        if k < 2:
+            window[k, previous] = (local_window[previous, :] + arrived(0) + arrived(1)).astype(BF16)
+            window[k, own] = v[k].astype(BF16)
+            window[k, following] = (local_window[following, :] + arrived(4) + arrived(5)).astype(
+                BF16
+            )
+
+    send_contribs(0, picked)
 
     place_t = as_column(place.astype(F32))
 
@@ -281,24 +286,22 @@
 
     lax.fori_loop(0, SLOTS // CASES, build_pick_t, 0)
     loads[4].wait()
-    corner_t[...] = jnp.transpose(corner[...].astype(F32)).astype(BF16)
-    high, low = two_parts(dot(pick[...], corner[...]))
+    reach = dot(pick[...], corner[...])
+    high, low = two_parts(reach)
     corner_w[:, :CORNERS] = high
     corner_w[:, CORNERS:] = low
+    high, low = two_parts(jnp.transpose(reach))
+    corner_t[:, :SLOTS] = high
+    corner_t[:, SLOTS:] = low
     loads[5].wait()
     loads[6].wait()
 
-    v[0] = assembled(0, own_part)
+    receive_contribs(0)
     for k in range(2):
-        window[k, own] = v[k].astype(BF16)
-        for copy in halo_copies(k):
-            copy.start()
+        w_part[k] = dot(corner_t[:, :SLOTS], window[k]) + dot(corner_t[:, SLOTS:], window[k])
+        chip_copy(k).start()
         norm = column_sum(v[k] * v[k])
-        for copy in halo_copies(k):
-            copy.wait_recv()
         u = dot(pick_t[...], window[k]).astype(BF16)
-        w_part[k] = dot(corner_t[...], u)
-        chip_copy(k).start()
         y = dot(dual[...], u)
         ring_sums = sum_rows(norm, column_sum(u.astype(F32) * y))
         chip_copy(k).wait_recv()
@@ -312,7 +315,7 @@
         split[:, CASES:] = low
         for block in (previous, own, following):
             local_window[block, :] = picked(block)
-        for d, copy in enumerate(ring_copies(k)):
+        for copy in ring_copies(k):
             copy.wait_recv()
         for d in range(chips - 1):
             half = half + ring_in[k, d, :HALF].astype(F32)
@@ -332,17 +335,13 @@
         def image(rows):
             return local_window[rows, :] + dot(corner_w[rows, :], z_twice)
 
-        contrib_out[k + 1, 0] = image(previous).astype(CONTRIB)
-        contrib_out[k + 1, 1] = image(following).astype(CONTRIB)
-        for copy in contrib_copies(k + 1):
-            copy.start()
+        send_contribs(k + 1, image)
         coarse = column_sum(w * z_narrow.astype(F32))
         totals[k, 0] = jnp.concatenate(
             [column_sum(ring_sums[0:3]), column_sum(ring_sums[3:6]) + coarse], axis=0
         )
         each_total(k, lambda copy: copy.start())
-        own_part = image(own)
-        v[k + 1] = assembled(k + 1, own_part)
+        receive_contribs(k + 1)
 
     for k in range(2):
         each_total(k, lambda copy: copy.wait_recv())
@@ -363,10 +362,10 @@
     residual_ref[...] = residual1 - alpha1 * (grown * v1 - alpha0 * v2)
 
     for k in range(3):
-        for copy in contrib_copies(k):
-            copy.wait_send()
+        for i in used_routes(k):
+            contrib_copy(k, i).wait_send()
     for k in range(2):
-        for copy in halo_copies(k) + [chip_copy(k), pair_copy(k)] + ring_copies(k):
+        for copy in [chip_copy(k), pair_copy(k)] + ring_copies(k):
             copy.wait_send()
         each_total(k, lambda copy: copy.wait_send())
 
@@ -376,7 +375,7 @@
     chips = subs // 2
     vmem = pl.BlockSpec(memory_space=pltpu.VMEM)
     smem = pl.BlockSpec(memory_space=pltpu.SMEM)
-    hbm = pl.BlockSpec(memory_space=pl.ANY)
+    hbm = pl.BlockSpec(memory_space=pltpu.HBM)
     dma = pltpu.SemaphoreType.DMA
 
     def on_device(
@@ -408,14 +407,14 @@
                 pltpu.VMEM((CORNERS, CORNERS), F32),
                 pltpu.VMEM((SLOTS, SLOTS), BF16),
                 pltpu.VMEM((SLOTS, SLOTS), BF16),
-                pltpu.VMEM((CORNERS, SLOTS), BF16),
+                pltpu.VMEM((CORNERS, 2 * SLOTS), BF16),
                 pltpu.VMEM((SLOTS, 2 * CORNERS), BF16),
                 pltpu.VMEM((SLOTS, 2 * CASES), BF16),
                 pltpu.VMEM((2, SLOTS, CASES), BF16),
                 pltpu.VMEM((SLOTS, CASES), F32),
                 pltpu.VMEM((3, OWN, CASES), F32),
-                pltpu.VMEM((3, 2, OWN, CASES), CONTRIB),
-                pltpu.VMEM((3, 2, OWN, CASES), CONTRIB),
+                pltpu.VMEM((3, 3, OWN, CASES), CONTRIB),
+                pltpu.VMEM((3, 6, OWN, CASES), CONTRIB),
                 pltpu.VMEM((2, CORNERS, CASES), F32),
                 pltpu.VMEM((CORNERS, CASES), F32),
                 pltpu.VMEM((2, HALF, CASES), F32),
@@ -425,10 +424,8 @@
                 pltpu.VMEM((2, HALF + SUMS, CASES), F32),
                 pltpu.VMEM((2, spans, 2, CASES), F32),
                 dma((7,)),
-                dma((3, 2)),
-                dma((3, 2)),
-                dma((2, 2)),
-                dma((2, 2)),
+                dma((3, 6)),
+                dma((3, 6)),
                 dma((2, 2)),
                 dma((2, chips - 1)),
                 dma((2, chips - 1)),
@@ -437,7 +434,7 @@
                 dma((2, spans)),
             ],
             compiler_params=pltpu.CompilerParams(
-                collective_id=0, has_side_effects=True, vmem_limit_bytes=32 * 2**20
+                collective_id=0, has_side_effects=True, vmem_limit_bytes=60 * 2**20
             ),
         )(
             retard,

time: 76.5 us -> 67.6 us (0.88)
  local copies, waits for them, and re-layouts: 8.68 us -> 3.14 us
  Pallas kernels: 66.1 us -> 63 us
    unnamed x20 -> x2, local copies, waits for them, and re-layouts: 8.68 us -> 3.14 us
    pallas_call x1, Pallas kernels: 66.1 us -> 63 us  [on_device(): pl.pallas_call(functools.partial(kernel, spans, subs), name='creep_step',...]
where the time goes in v2:
time: 67.6 us; the launch traced here: 67.4 us
  Pallas kernels  63 us (93%)
  local copies, waits for them, and re-layouts  3.14 us (5%)
  between operations  1.29 us (2%)
    pallas_call x1, Pallas kernels, on_device(): pl.pallas_call(functools.partial(kernel, spans, subs), name='creep_step',...  63 us
    unnamed x2, local copies, waits for them, and re-layouts  3.14 us

profile of v2, /device:TPU:1, one launch (start us, length us, event | category | flops | bytes accessed | tf_op | source)
XLA Modules:
  0.0 67.4 jit_solution(7995822697253324963)
XLA Ops:
  1.3 63.0 %creep_step.1 = (f32[256,128]{1,0:T(8,128)}, f32[256,128]{1,0:T(8,128)}) custom-call(f32[8]{0:T(128)} %retard.1, f32[8]{0:T(128)} %compliance.1, s32[1]{0:T(128)S(6)} %copy.14.lengths, bf16[1,768,128]{2,1,0:T(8,128)(2,1)} %stress_hbm.1, f32[8,1,768]{2,1,0:T(1,128)} %history_hbm.1, f32[1,768]{1,0:T(1,128)} %micro_hbm.1, s32[1,768]{1,0:T(1,128)} %index_hbm.1, ...), custom_call_target="tpu_custom_call" | custom-call | tf_op jit(solution)/shard_map/creep_step/pallas_call | solution.py:394
  64.2 1.6 %copy.15 = f32[256,128]{1,0:T(8,128)} copy(f32[256,128]{1,0:T(8,128)} %get-tuple-element.4) | data formatting | bytes 262144
  65.8 1.6 %copy.16 = f32[256,128]{1,0:T(8,128)} copy(f32[256,128]{1,0:T(8,128)} %get-tuple-element.5) | data formatting | bytes 262144

commit v3 on v2

--- a/solution.py
+++ b/solution.py
@@ -52,9 +52,9 @@
 def kernel(
     spans,
     subs,
-    retard,
-    compliance,
-    lengths,
+    retard_hbm,
+    compliance_hbm,
+    lengths_hbm,
     stress_hbm,
     history_hbm,
     micro_hbm,
@@ -62,8 +62,14 @@
     dual_hbm,
     corner_hbm,
     stiff_hbm,
-    solution_ref,
-    residual_ref,
+    basis0_hbm,
+    basis1_hbm,
+    basis2_hbm,
+    factor0,
+    factor1,
+    retard,
+    compliance,
+    lengths,
     stress,
     history,
     micro,
@@ -90,14 +96,13 @@
     pair_in,
     totals,
     load_sem,
+    keep_sem,
     contrib_send,
     contrib_recv,
     chip_sem,
-    ring_send,
-    ring_recv,
+    ring_sem,
     pair_sem,
-    total_send,
-    total_recv,
+    total_sem,
 ):
     p = lax.axis_index("span")
     s = lax.axis_index("sub")
@@ -111,7 +116,10 @@
         pltpu.make_async_copy(src, dst, load_sem.at[i])
         for i, (src, dst) in enumerate(
             (
+                (lengths_hbm, lengths),
                 (index_hbm, index),
+                (retard_hbm, retard),
+                (compliance_hbm, compliance),
                 (micro_hbm, micro),
                 (history_hbm, history),
                 (stress_hbm.at[0], stress),
@@ -143,10 +151,11 @@
     pl.semaphore_signal(barrier, inc=1, device_id=partner, device_id_type=MESH)
 
     loads[0].wait()
+    loads[1].wait()
     slot = lax.broadcasted_iota(jnp.int32, (1, SLOTS), 1)
     owner_span = index[...] // (OWN * subs)
     place = (owner_span - p + 1) * OWN + lax.rem(index[...], OWN)
-    place = jnp.where(slot < lengths[0], place, -1)
+    place = jnp.where(slot < lengths[0, 0], place, -1)
 
     def build_pick(i, carry):
         rows = pl.ds(pl.multiple_of(i * ROWS, ROWS), ROWS)
@@ -156,8 +165,8 @@
 
     lax.fori_loop(0, SLOTS // ROWS, build_pick, 0)
 
-    loads[1].wait()
-    loads[2].wait()
+    for copy in loads[2:6]:
+        copy.wait()
     creep = jnp.zeros((1, SLOTS), F32)
     past = jnp.zeros((1, SLOTS), F32)
     for k in range(history.shape[0]):
@@ -167,7 +176,7 @@
     relaxed = micro[...] / (1.0 + micro[...])
     scale = as_column(creep + 0.5 * relaxed)
     past = as_column(past)
-    loads[3].wait()
+    loads[6].wait()
     load = scale * stress[...].astype(F32) - past
     high, low = two_parts(load)
     split[:, :CASES] = high
@@ -208,13 +217,23 @@
             pltpu.make_async_remote_copy(
                 src_ref=ring_out.at[k],
                 dst_ref=ring_in.at[k, d - 1],
-                send_sem=ring_send.at[k, d - 1],
-                recv_sem=ring_recv.at[k, d - 1],
+                send_sem=ring_sem.at[k, 0],
+                recv_sem=ring_sem.at[k, 1],
                 device_id=(p, lax.rem(s + 2 * d, subs)),
                 device_id_type=MESH,
             )
             for d in range(1, chips)
         ]
+
+    def all_ring(k):
+        return pltpu.make_async_remote_copy(
+            src_ref=ring_in.at[k],
+            dst_ref=ring_in.at[k],
+            send_sem=ring_sem.at[k, 0],
+            recv_sem=ring_sem.at[k, 1],
+            device_id=partner,
+            device_id_type=MESH,
+        )
 
     def pair_copy(k):
         return pltpu.make_async_remote_copy(
@@ -230,18 +249,29 @@
         return pltpu.make_async_remote_copy(
             src_ref=totals.at[k, 0],
             dst_ref=totals.at[k, d],
-            send_sem=total_send.at[k, d],
-            recv_sem=total_recv.at[k, d],
+            send_sem=total_sem.at[k, 0],
+            recv_sem=total_sem.at[k, 1],
             device_id=(lax.rem(p + d, spans), s),
             device_id_type=MESH,
         )
 
-    def each_total(k, act):
+    def send_totals(k):
         def step(d, carry):
-            act(total_copy(k, d))
+            total_copy(k, d).start()
             return carry
 
         lax.fori_loop(1, spans, step, 0)
+
+    def all_totals(k):
+        rest = totals.at[k, pl.ds(1, spans - 1)]
+        return pltpu.make_async_remote_copy(
+            src_ref=rest,
+            dst_ref=rest,
+            send_sem=total_sem.at[k, 0],
+            recv_sem=total_sem.at[k, 1],
+            device_id=partner,
+            device_id_type=MESH,
+        )
 
     previous, own, following = blocks = [slice(i * OWN, (i + 1) * OWN) for i in range(3)]
 
@@ -256,8 +286,6 @@
             for i in reversed(used_routes(k)):
                 if routes[i][0] == block:
                     contrib_copy(k, i).start()
-        if k == 2:
-            local_window[own, :] = image(own)
 
     def receive_contribs(k):
         for i in used_routes(k):
@@ -267,6 +295,7 @@
             return contrib_in[k, i].astype(F32)
 
         v[k] = local_window[own, :] + arrived(2) + arrived(3)
+        keeps[k].start()
         if k < 2:
             window[k, previous] = (local_window[previous, :] + arrived(0) + arrived(1)).astype(BF16)
             window[k, own] = v[k].astype(BF16)
@@ -274,6 +303,10 @@
                 BF16
             )
 
+    keeps = [
+        pltpu.make_async_copy(v.at[k], out, keep_sem.at[k])
+        for k, out in enumerate((basis0_hbm, basis1_hbm, basis2_hbm))
+    ]
     send_contribs(0, picked)
 
     place_t = as_column(place.astype(F32))
@@ -285,20 +318,21 @@
         return carry
 
     lax.fori_loop(0, SLOTS // CASES, build_pick_t, 0)
-    loads[4].wait()
+    loads[7].wait()
     reach = dot(pick[...], corner[...])
     high, low = two_parts(reach)
     corner_w[:, :CORNERS] = high
     corner_w[:, CORNERS:] = low
     high, low = two_parts(jnp.transpose(reach))
-    corner_t[:, :SLOTS] = high
-    corner_t[:, SLOTS:] = low
-    loads[5].wait()
-    loads[6].wait()
+    corner_t[:CORNERS, :] = high
+    corner_t[CORNERS:, :] = low
+    loads[8].wait()
+    loads[9].wait()
 
     receive_contribs(0)
     for k in range(2):
-        w_part[k] = dot(corner_t[:, :SLOTS], window[k]) + dot(corner_t[:, SLOTS:], window[k])
+        both = dot(corner_t[...], window[k])
+        w_part[k] = both[:CORNERS] + both[CORNERS:]
         chip_copy(k).start()
         norm = column_sum(v[k] * v[k])
         u = dot(pick_t[...], window[k]).astype(BF16)
@@ -315,8 +349,7 @@
         split[:, CASES:] = low
         for block in (previous, own, following):
             local_window[block, :] = picked(block)
-        for copy in ring_copies(k):
-            copy.wait_recv()
+        all_ring(k).wait_recv()
         for d in range(chips - 1):
             half = half + ring_in[k, d, :HALF].astype(F32)
             ring_sums = ring_sums + ring_in[k, d, HALF:].astype(F32)
@@ -340,11 +373,13 @@
         totals[k, 0] = jnp.concatenate(
             [column_sum(ring_sums[0:3]), column_sum(ring_sums[3:6]) + coarse], axis=0
         )
-        each_total(k, lambda copy: copy.start())
+        send_totals(k)
+        if k == 1:
+            local_window[own, :] = image(own)
         receive_contribs(k + 1)
 
     for k in range(2):
-        each_total(k, lambda copy: copy.wait_recv())
+        all_totals(k).wait_recv()
     first = jnp.sum(totals[0], axis=0)
     second = jnp.sum(totals[1], axis=0)
     g00, g01 = first[0:1], first[1:2]
@@ -355,27 +390,25 @@
     grown = 1.0 + beta
     curve = grown * grown * g01 - 2.0 * grown * alpha0 * g11 + alpha0 * alpha0 * g12
     alpha1 = norm1 / curve
-    v0, v1, v2 = v[0], v[1], v[2]
-    residual1 = v0 - alpha0 * v1
-    direction1 = residual1 + beta * v0
-    solution_ref[...] = alpha0 * v0 + alpha1 * direction1
-    residual_ref[...] = residual1 - alpha1 * (grown * v1 - alpha0 * v2)
+    factor0[...] = alpha0 + alpha1 * grown
+    factor1[...] = alpha0 * alpha1
+    for copy in keeps:
+        copy.wait()
 
     for k in range(3):
         for i in used_routes(k):
             contrib_copy(k, i).wait_send()
     for k in range(2):
-        for copy in [chip_copy(k), pair_copy(k)] + ring_copies(k):
+        for copy in (chip_copy(k), pair_copy(k), all_ring(k)):
             copy.wait_send()
-        each_total(k, lambda copy: copy.wait_send())
+        all_totals(k).wait_send()
 
 
 def solution(mesh):
     spans, subs = mesh.shape["span"], mesh.shape["sub"]
     chips = subs // 2
     vmem = pl.BlockSpec(memory_space=pltpu.VMEM)
-    smem = pl.BlockSpec(memory_space=pltpu.SMEM)
-    hbm = pl.BlockSpec(memory_space=pltpu.HBM)
+    hbm = pl.BlockSpec(memory_space=pl.ANY)
     dma = pltpu.SemaphoreType.DMA
 
     def on_device(
@@ -391,13 +424,17 @@
         coarse_stiffness_inverse,
     ):
         units = history.shape[0]
-        return pl.pallas_call(
+        v0, v1, v2, first, second = pl.pallas_call(
             functools.partial(kernel, spans, subs),
             name="creep_step",
-            out_shape=[jax.ShapeDtypeStruct((OWN, CASES), F32)] * 2,
-            in_specs=[smem] * 3 + [hbm] * 7,
-            out_specs=[vmem] * 2,
+            out_shape=[jax.ShapeDtypeStruct((OWN, CASES), F32)] * 3
+            + [jax.ShapeDtypeStruct((1, CASES), F32)] * 2,
+            in_specs=[hbm] * 10,
+            out_specs=[hbm] * 3 + [vmem] * 2,
             scratch_shapes=[
+                pltpu.SMEM((units,), F32),
+                pltpu.SMEM((units,), F32),
+                pltpu.SMEM((1, 1), jnp.int32),
                 pltpu.VMEM((SLOTS, CASES), BF16),
                 pltpu.VMEM((units, 1, SLOTS), F32),
                 pltpu.VMEM((1, SLOTS), F32),
@@ -407,7 +444,7 @@
                 pltpu.VMEM((CORNERS, CORNERS), F32),
                 pltpu.VMEM((SLOTS, SLOTS), BF16),
                 pltpu.VMEM((SLOTS, SLOTS), BF16),
-                pltpu.VMEM((CORNERS, 2 * SLOTS), BF16),
+                pltpu.VMEM((2 * CORNERS, SLOTS), BF16),
                 pltpu.VMEM((SLOTS, 2 * CORNERS), BF16),
                 pltpu.VMEM((SLOTS, 2 * CASES), BF16),
                 pltpu.VMEM((2, SLOTS, CASES), BF16),
@@ -423,15 +460,14 @@
                 pltpu.VMEM((2, HALF + SUMS, CASES), F32),
                 pltpu.VMEM((2, HALF + SUMS, CASES), F32),
                 pltpu.VMEM((2, spans, 2, CASES), F32),
-                dma((7,)),
+                dma((10,)),
+                dma((3,)),
                 dma((3, 6)),
                 dma((3, 6)),
                 dma((2, 2)),
-                dma((2, chips - 1)),
-                dma((2, chips - 1)),
                 dma((2, 2)),
-                dma((2, spans)),
-                dma((2, spans)),
+                dma((2, 2)),
+                dma((2, 2)),
             ],
             compiler_params=pltpu.CompilerParams(
                 collective_id=0, has_side_effects=True, vmem_limit_bytes=60 * 2**20
@@ -439,7 +475,7 @@
         )(
             retard,
             compliance,
-            lengths,
+            lengths.reshape(1, 1),
             stress,
             history,
             micro,
@@ -448,6 +484,7 @@
             corner_map,
             coarse_stiffness_inverse,
         )
+        return first * v0 - second * v1, v0 - first * v1 + second * v2
 
     rows = P(("span", "sub"), None)
     blocks = P(("span", "sub"), None, None)

time: 67.6 us -> 63.7 us (0.942)
  local copies, waits for them, and re-layouts: 3.14 us -> 0 us
  Pallas kernels: 63 us -> 60.4 us
  other arithmetic: 0 us -> 1.77 us
    unnamed x2 -> x0, local copies, waits for them, and re-layouts: 3.14 us -> none
    pallas_call x1, Pallas kernels: 63 us -> 60.4 us  [on_device(): pl.pallas_call(functools.partial(kernel, spans, subs), name='creep_step',...]
    add x0 -> x1, other arithmetic: none -> 1.77 us  [on_device(): return (first * v0 - second * v1, v0 - first * v1 + second * v2)]
where the time goes in v3:
time: 63.7 us; the launch traced here: 63.5 us
  Pallas kernels  60.4 us (95%)
  other arithmetic  1.77 us (3%)
  between operations  1.29 us (2%)
    pallas_call x1, Pallas kernels, on_device(): pl.pallas_call(functools.partial(kernel, spans, subs), name='creep_step',...  60.4 us
    add x1, other arithmetic, on_device(): return (first * v0 - second * v1, v0 - first * v1 + second * v2)  1.77 us

profile of v3, /device:TPU:1, one launch (start us, length us, event | category | flops | bytes accessed | tf_op | source)
XLA Modules:
  0.0 63.5 jit_solution(14428896646749432987)
XLA Ops:
  1.3 60.4 %creep_step.1 = (f32[256,128]{1,0:T(8,128)}, f32[256,128]{1,0:T(8,128)}, f32[256,128]{1,0:T(8,128)}, f32[1,128]{1,0:T(1,128)}, f32[1,128]{1,0:T(1,128)}) custom-call(f32[8]{0:T(128)} %retard_hbm.1, f32[8]{0:T(128)} %compliance_hbm.1, s32[1,1]{1,0:T(1,128)} %bitcast.3.lengths_hbm, bf16[1,768,128]{2,1,0:T(8,128)(2,1)} %stress_hbm.1, f32[8,1,768]{2,1,0:T(1,128)} %history_hbm.1, ...), custom_call_target="tpu_custom_call" | custom-call | tf_op jit(solution)/shard_map/creep_step/pallas_call | solution.py:427
  61.7 1.8 %multiply_add_fusion = (f32[256,128]{1,0:T(8,128)}, f32[256,128]{1,0:T(8,128)}) fusion(f32[256,128]{1,0:T(8,128)} %get-tuple-element.11, f32[256,128]{1,0:T(8,128)} %get-tuple-element.8, f32[256,128]{1,0:T(8,128)} %get-tuple-element.10, f32[128]{0:T(128)} %bitcast.5, f32[128]{0:T(128)} %bitcast.4), kind=kLoop, calls=%fused_computation | loop fusion | flops 229376 | bytes 656384 | tf_op jit(solution)/shard_map/add | solution.py:487

commit v4 on v3

--- a/solution.py
+++ b/solution.py
@@ -81,6 +81,8 @@
     pick_t,
     corner_t,
     corner_w,
+    coarse,
+    w_near,
     split,
     window,
     local_window,
@@ -99,6 +101,10 @@
     keep_sem,
     contrib_send,
     contrib_recv,
+    coarse_send,
+    coarse_recv,
+    near_send,
+    near_recv,
     chip_sem,
     ring_sem,
     pair_sem,
@@ -146,9 +152,14 @@
         )
         return carry
 
-    lax.fori_loop(1, spans, greet_span, 0)
+    pl.semaphore_signal(barrier, inc=1, device_id=partner, device_id_type=MESH)
+    for d in (1, spans - 1, 2, spans - 2):
+        greet_span(d, 0)
+        pl.semaphore_signal(
+            barrier, inc=1, device_id=(lax.rem(p + d, spans), partner[1]), device_id_type=MESH
+        )
     lax.fori_loop(1, chips, greet_chip, 0)
-    pl.semaphore_signal(barrier, inc=1, device_id=partner, device_id_type=MESH)
+    lax.fori_loop(3, spans - 2, greet_span, 0)
 
     loads[0].wait()
     loads[1].wait()
@@ -199,6 +210,49 @@
             device_id_type=MESH,
         )
 
+    landing = ((0, 1), (0, 0), (1, 0), (1, 2), (2, 1), (2, 2))
+
+    def coarse_copy(i):
+        block, onward = routes[i]
+        row, column = landing[i]
+        return pltpu.make_async_remote_copy(
+            src_ref=coarse.at[pl.ds(block * OWN, OWN), pl.ds((2 - block) * CORNERS, CORNERS)],
+            dst_ref=coarse.at[pl.ds(row * OWN, OWN), pl.ds(column * CORNERS, CORNERS)],
+            send_sem=coarse_send.at[i],
+            recv_sem=coarse_recv.at[i],
+            device_id=(lax.rem(p + spans + onward, spans), s),
+            device_id_type=MESH,
+        )
+
+    def near_copies():
+        kept = w_near.at[pl.ds(pl.multiple_of(2 * CORNERS + core * HALF, HALF), HALF)]
+        copies = []
+        for onward in (2, -2, 1, -1):
+            place = pl.multiple_of((2 - onward) * CORNERS + core * HALF, HALF)
+            for to in (s, partner[1]):
+                copies.append(
+                    pltpu.make_async_remote_copy(
+                        src_ref=kept,
+                        dst_ref=w_near.at[pl.ds(place, HALF)],
+                        send_sem=near_send.at[len(copies)],
+                        recv_sem=near_recv.at[0 if onward > 0 else 1],
+                        device_id=(lax.rem(p + spans + onward, spans), to),
+                        device_id_type=MESH,
+                    )
+                )
+        return copies
+
+    def all_near(side):
+        rows = w_near.at[pl.ds(side * 3 * CORNERS, 2 * CORNERS)]
+        return pltpu.make_async_remote_copy(
+            src_ref=rows,
+            dst_ref=rows,
+            send_sem=near_send.at[0],
+            recv_sem=near_recv.at[side],
+            device_id=partner,
+            device_id_type=MESH,
+        )
+
     def used_routes(k):
         return range(6) if k < 2 else (2, 3)
 
@@ -282,7 +336,7 @@
                 local_window[blocks[block], :] = value
             contrib_out[k, block] = value.astype(CONTRIB)
             if k == 0 and block == 0:
-                pl.semaphore_wait(barrier, spans + chips - 1)
+                pl.semaphore_wait(barrier, spans + chips + 3)
             for i in reversed(used_routes(k)):
                 if routes[i][0] == block:
                     contrib_copy(k, i).start()
@@ -294,6 +348,14 @@
         def arrived(i):
             return contrib_in[k, i].astype(F32)
 
+        if k == 1:
+            for i in used_routes(k):
+                coarse_copy(i).wait_recv()
+            for side in range(2):
+                all_near(side).wait_recv()
+            for block in range(3):
+                near = w_near[block * CORNERS : (block + 3) * CORNERS, :]
+                local_window[blocks[block], :] += dot(coarse[blocks[block], :], near)
         v[k] = local_window[own, :] + arrived(2) + arrived(3)
         keeps[k].start()
         if k < 2:
@@ -309,26 +371,33 @@
     ]
     send_contribs(0, picked)
 
-    place_t = as_column(place.astype(F32))
-
-    def build_pick_t(j, carry):
-        lanes = pl.ds(pl.multiple_of(j * CASES, CASES), CASES)
-        at = lax.broadcasted_iota(jnp.int32, (SLOTS, CASES), 1) + j * CASES
-        pick_t[:, lanes] = jnp.where(place_t == at.astype(F32), 1.0, 0.0).astype(BF16)
-        return carry
-
-    lax.fori_loop(0, SLOTS // CASES, build_pick_t, 0)
     loads[7].wait()
     reach = dot(pick[...], corner[...])
+    loads[9].wait()
+    spread = jnp.dot(reach, stiff[...], precision=lax.Precision.HIGHEST, preferred_element_type=F32)
+    for block in range(3):
+        coarse[blocks[block], (2 - block) * CORNERS : (3 - block) * CORNERS] = spread[
+            blocks[block]
+        ].astype(BF16)
+
+    for i in reversed(used_routes(0)):
+        coarse_copy(i).start()
     high, low = two_parts(reach)
     corner_w[:, :CORNERS] = high
     corner_w[:, CORNERS:] = low
     high, low = two_parts(jnp.transpose(reach))
     corner_t[:CORNERS, :] = high
     corner_t[CORNERS:, :] = low
+    place_t = as_column(place.astype(F32))
+
+    def build_pick_t(j, carry):
+        lanes = pl.ds(pl.multiple_of(j * CASES, CASES), CASES)
+        at = lax.broadcasted_iota(jnp.int32, (SLOTS, CASES), 1) + j * CASES
+        pick_t[:, lanes] = jnp.where(place_t == at.astype(F32), 1.0, 0.0).astype(BF16)
+        return carry
+
+    lax.fori_loop(0, SLOTS // CASES, build_pick_t, 0)
     loads[8].wait()
-    loads[9].wait()
-
     receive_contribs(0)
     for k in range(2):
         both = dot(corner_t[...], window[k])
@@ -347,8 +416,11 @@
         high, low = two_parts(y)
         split[:, :CASES] = high
         split[:, CASES:] = low
-        for block in (previous, own, following):
-            local_window[block, :] = picked(block)
+        if k == 0:
+            send_contribs(1, picked)
+        else:
+            for block in blocks:
+                local_window[block, :] = picked(block)
         all_ring(k).wait_recv()
         for d in range(chips - 1):
             half = half + ring_in[k, d, :HALF].astype(F32)
@@ -356,9 +428,19 @@
         pair_out[k, :HALF] = half
         pair_out[k, HALF:] = ring_sums
         pair_copy(k).start()
+        if k == 0:
+            w_near[pl.ds(pl.multiple_of(2 * CORNERS + core * HALF, HALF), HALF), :] = half.astype(
+                BF16
+            )
+            for copy in near_copies():
+                copy.start()
         w_full[mine, :] = half
         pair_copy(k).wait_recv()
         w_full[theirs, :] = pair_in[k, :HALF]
+        if k == 0:
+            w_near[pl.ds(pl.multiple_of(3 * CORNERS - HALF - core * HALF, HALF), HALF), :] = pair_in[
+                k, :HALF
+            ].astype(BF16)
         ring_sums = ring_sums + pair_in[k, HALF:]
         w = w_full[...]
         z = jnp.dot(stiff[...], w, precision=lax.Precision.HIGHEST, preferred_element_type=F32)
@@ -368,10 +450,11 @@
         def image(rows):
             return local_window[rows, :] + dot(corner_w[rows, :], z_twice)
 
-        send_contribs(k + 1, image)
-        coarse = column_sum(w * z_narrow.astype(F32))
+        if k == 1:
+            send_contribs(2, image)
+        energy = column_sum(w * z_narrow.astype(F32))
         totals[k, 0] = jnp.concatenate(
-            [column_sum(ring_sums[0:3]), column_sum(ring_sums[3:6]) + coarse], axis=0
+            [column_sum(ring_sums[0:3]), column_sum(ring_sums[3:6]) + energy], axis=0
         )
         send_totals(k)
         if k == 1:
@@ -395,11 +478,12 @@
     for copy in keeps:
         copy.wait()
 
+    tail = near_copies() + [coarse_copy(i) for i in range(6)]
     for k in range(3):
         for i in used_routes(k):
             contrib_copy(k, i).wait_send()
     for k in range(2):
-        for copy in (chip_copy(k), pair_copy(k), all_ring(k)):
+        for copy in [chip_copy(k), pair_copy(k), all_ring(k)] + (tail if k == 0 else []):
             copy.wait_send()
         all_totals(k).wait_send()
 
@@ -446,6 +530,8 @@
                 pltpu.VMEM((SLOTS, SLOTS), BF16),
                 pltpu.VMEM((2 * CORNERS, SLOTS), BF16),
                 pltpu.VMEM((SLOTS, 2 * CORNERS), BF16),
+                pltpu.VMEM((SLOTS, 3 * CORNERS), BF16),
+                pltpu.VMEM((5 * CORNERS, CASES), BF16),
                 pltpu.VMEM((SLOTS, 2 * CASES), BF16),
                 pltpu.VMEM((2, SLOTS, CASES), BF16),
                 pltpu.VMEM((SLOTS, CASES), F32),
@@ -464,6 +550,10 @@
                 dma((3,)),
                 dma((3, 6)),
                 dma((3, 6)),
+                dma((6,)),
+                dma((6,)),
+                dma((8,)),
+                dma((2,)),
                 dma((2, 2)),
                 dma((2, 2)),
                 dma((2, 2)),

time: 63.7 us -> 62 us (0.973)
  Pallas kernels: 60.4 us -> 58.7 us
    pallas_call x1, Pallas kernels: 60.4 us -> 58.7 us  [on_device(): pl.pallas_call(functools.partial(kernel, spans, subs), name='creep_step',...]
where the time goes in v4:
time: 62 us; the launch traced here: 61.8 us
  Pallas kernels  58.7 us (95%)
  other arithmetic  1.77 us (3%)
  between operations  1.29 us (2%)
    pallas_call x1, Pallas kernels, on_device(): pl.pallas_call(functools.partial(kernel, spans, subs), name='creep_step',...  58.7 us
    add x1, other arithmetic, on_device(): return (first * v0 - second * v1, v0 - first * v1 + second * v2)  1.77 us

profile of v4, /device:TPU:1, one launch (start us, length us, event | category | flops | bytes accessed | tf_op | source)
XLA Modules:
  0.0 61.8 jit_solution(13804983856949056070)
XLA Ops:
  1.3 58.7 %creep_step.1 = (f32[256,128]{1,0:T(8,128)}, f32[256,128]{1,0:T(8,128)}, f32[256,128]{1,0:T(8,128)}, f32[1,128]{1,0:T(1,128)}, f32[1,128]{1,0:T(1,128)}) custom-call(f32[8]{0:T(128)} %retard_hbm.1, f32[8]{0:T(128)} %compliance_hbm.1, s32[1,1]{1,0:T(1,128)} %bitcast.3.lengths_hbm, bf16[1,768,128]{2,1,0:T(8,128)(2,1)} %stress_hbm.1, f32[8,1,768]{2,1,0:T(1,128)} %history_hbm.1, ...), custom_call_target="tpu_custom_call" | custom-call | tf_op jit(solution)/shard_map/creep_step/pallas_call | solution.py:511
  60.0 1.8 %multiply_add_fusion = (f32[256,128]{1,0:T(8,128)}, f32[256,128]{1,0:T(8,128)}) fusion(f32[256,128]{1,0:T(8,128)} %get-tuple-element.11, f32[256,128]{1,0:T(8,128)} %get-tuple-element.8, f32[256,128]{1,0:T(8,128)} %get-tuple-element.10, f32[128]{0:T(128)} %bitcast.5, f32[128]{0:T(128)} %bitcast.4), kind=kLoop, calls=%fused_computation | loop fusion | flops 229376 | bytes 656384 | tf_op jit(solution)/shard_map/add | solution.py:577

commit v5 on v4

--- a/solution.py
+++ b/solution.py
@@ -276,7 +276,7 @@
                 device_id=(p, lax.rem(s + 2 * d, subs)),
                 device_id_type=MESH,
             )
-            for d in range(1, chips)
+            for d in sorted(range(1, chips), key=lambda d: -min(d, chips - d))
         ]
 
     def all_ring(k):
@@ -299,30 +299,28 @@
             device_id_type=MESH,
         )
 
-    def total_copy(k, d):
-        return pltpu.make_async_remote_copy(
-            src_ref=totals.at[k, 0],
-            dst_ref=totals.at[k, d],
-            send_sem=total_sem.at[k, 0],
-            recv_sem=total_sem.at[k, 1],
-            device_id=(lax.rem(p + d, spans), s),
-            device_id_type=MESH,
-        )
-
-    def send_totals(k):
-        def step(d, carry):
-            total_copy(k, d).start()
+    def send_totals():
+        def step(i, carry):
+            d = 1 + lax.rem(i + spans // 3, spans - 1)
+            pltpu.make_async_remote_copy(
+                src_ref=totals.at[0],
+                dst_ref=totals.at[d],
+                send_sem=total_sem.at[0],
+                recv_sem=total_sem.at[1],
+                device_id=(lax.rem(p + d, spans), s),
+                device_id_type=MESH,
+            ).start()
             return carry
 
-        lax.fori_loop(1, spans, step, 0)
-
-    def all_totals(k):
-        rest = totals.at[k, pl.ds(1, spans - 1)]
+        lax.fori_loop(0, spans - 1, step, 0)
+
+    def all_totals():
+        rest = totals.at[pl.ds(1, spans - 1)]
         return pltpu.make_async_remote_copy(
             src_ref=rest,
             dst_ref=rest,
-            send_sem=total_sem.at[k, 0],
-            recv_sem=total_sem.at[k, 1],
+            send_sem=total_sem.at[0],
+            recv_sem=total_sem.at[1],
             device_id=partner,
             device_id_type=MESH,
         )
@@ -337,7 +335,7 @@
             contrib_out[k, block] = value.astype(CONTRIB)
             if k == 0 and block == 0:
                 pl.semaphore_wait(barrier, spans + chips + 3)
-            for i in reversed(used_routes(k)):
+            for i in sorted(used_routes(k), key=lambda i: -abs(routes[i][1])):
                 if routes[i][0] == block:
                     contrib_copy(k, i).start()
 
@@ -453,20 +451,17 @@
         if k == 1:
             send_contribs(2, image)
         energy = column_sum(w * z_narrow.astype(F32))
-        totals[k, 0] = jnp.concatenate(
-            [column_sum(ring_sums[0:3]), column_sum(ring_sums[3:6]) + energy], axis=0
-        )
-        send_totals(k)
+        totals[0, 2 * k : 2 * k + 1] = column_sum(ring_sums[0:3])
+        totals[0, 2 * k + 1 : 2 * k + 2] = column_sum(ring_sums[3:6]) + energy
+        if k == 1:
+            send_totals()
         if k == 1:
             local_window[own, :] = image(own)
         receive_contribs(k + 1)
 
-    for k in range(2):
-        all_totals(k).wait_recv()
-    first = jnp.sum(totals[0], axis=0)
-    second = jnp.sum(totals[1], axis=0)
-    g00, g01 = first[0:1], first[1:2]
-    g11, g12 = second[0:1], second[1:2]
+    all_totals().wait_recv()
+    products = jnp.sum(totals[...], axis=0)
+    g00, g01, g11, g12 = (products[i : i + 1] for i in range(4))
     alpha0 = g00 / g01
     norm1 = g00 - 2.0 * alpha0 * g01 + alpha0 * alpha0 * g11
     beta = norm1 / g00
@@ -477,6 +472,7 @@
     factor1[...] = alpha0 * alpha1
     for copy in keeps:
         copy.wait()
+    all_totals().wait_send()
 
     tail = near_copies() + [coarse_copy(i) for i in range(6)]
     for k in range(3):
@@ -485,7 +481,6 @@
     for k in range(2):
         for copy in [chip_copy(k), pair_copy(k), all_ring(k)] + (tail if k == 0 else []):
             copy.wait_send()
-        all_totals(k).wait_send()
 
 
 def solution(mesh):
@@ -545,7 +540,7 @@
                 pltpu.VMEM((2, chips - 1, HALF + SUMS, CASES), BF16),
                 pltpu.VMEM((2, HALF + SUMS, CASES), F32),
                 pltpu.VMEM((2, HALF + SUMS, CASES), F32),
-                pltpu.VMEM((2, spans, 2, CASES), F32),
+                pltpu.VMEM((spans, 4, CASES), F32),
                 dma((10,)),
                 dma((3,)),
                 dma((3, 6)),
@@ -557,7 +552,7 @@
                 dma((2, 2)),
                 dma((2, 2)),
                 dma((2, 2)),
-                dma((2, 2)),
+                dma((2,)),
             ],
             compiler_params=pltpu.CompilerParams(
                 collective_id=0, has_side_effects=True, vmem_limit_bytes=60 * 2**20

time: 62 us -> 59.8 us (0.965)
  Pallas kernels: 58.7 us -> 56.6 us
    pallas_call x1, Pallas kernels: 58.7 us -> 56.6 us  [on_device(): pl.pallas_call(functools.partial(kernel, spans, subs), name='creep_step',...]
where the time goes in v5:
time: 59.8 us; the launch traced here: 59.7 us
  Pallas kernels  56.6 us (95%)
  other arithmetic  1.77 us (3%)
  between operations  1.29 us (2%)
    pallas_call x1, Pallas kernels, on_device(): pl.pallas_call(functools.partial(kernel, spans, subs), name='creep_step',...  56.6 us
    add x1, other arithmetic, on_device(): return (first * v0 - second * v1, v0 - first * v1 + second * v2)  1.77 us

profile of v5, /device:TPU:1, one launch (start us, length us, event | category | flops | bytes accessed | tf_op | source)
XLA Modules:
  0.0 59.7 jit_solution(17248005283818339377)
XLA Ops:
  1.3 56.6 %creep_step.1 = (f32[256,128]{1,0:T(8,128)}, f32[256,128]{1,0:T(8,128)}, f32[256,128]{1,0:T(8,128)}, f32[1,128]{1,0:T(1,128)}, f32[1,128]{1,0:T(1,128)}) custom-call(f32[8]{0:T(128)} %retard_hbm.1, f32[8]{0:T(128)} %compliance_hbm.1, s32[1,1]{1,0:T(1,128)} %bitcast.3.lengths_hbm, bf16[1,768,128]{2,1,0:T(8,128)(2,1)} %stress_hbm.1, f32[8,1,768]{2,1,0:T(1,128)} %history_hbm.1, ...), custom_call_target="tpu_custom_call" | custom-call | tf_op jit(solution)/shard_map/creep_step/pallas_call | solution.py:506
  57.9 1.8 %multiply_add_fusion = (f32[256,128]{1,0:T(8,128)}, f32[256,128]{1,0:T(8,128)}) fusion(f32[256,128]{1,0:T(8,128)} %get-tuple-element.11, f32[256,128]{1,0:T(8,128)} %get-tuple-element.8, f32[256,128]{1,0:T(8,128)} %get-tuple-element.10, f32[128]{0:T(128)} %bitcast.5, f32[128]{0:T(128)} %bitcast.4), kind=kLoop, calls=%fused_computation | loop fusion | flops 229376 | bytes 656384 | tf_op jit(solution)/shard_map/add | solution.py:572

commit v6 on v5

--- a/solution.py
+++ b/solution.py
@@ -62,9 +62,9 @@
     dual_hbm,
     corner_hbm,
     stiff_hbm,
-    basis0_hbm,
-    basis1_hbm,
-    basis2_hbm,
+    basis0,
+    basis1,
+    basis2,
     factor0,
     factor1,
     retard,
@@ -86,7 +86,6 @@
     split,
     window,
     local_window,
-    v,
     contrib_out,
     contrib_in,
     w_part,
@@ -98,7 +97,6 @@
     pair_in,
     totals,
     load_sem,
-    keep_sem,
     contrib_send,
     contrib_recv,
     coarse_send,
@@ -110,6 +108,7 @@
     pair_sem,
     total_sem,
 ):
+    basis = (basis0, basis1, basis2)
     p = lax.axis_index("span")
     s = lax.axis_index("sub")
     chips = subs // 2
@@ -354,19 +353,14 @@
             for block in range(3):
                 near = w_near[block * CORNERS : (block + 3) * CORNERS, :]
                 local_window[blocks[block], :] += dot(coarse[blocks[block], :], near)
-        v[k] = local_window[own, :] + arrived(2) + arrived(3)
-        keeps[k].start()
+        basis[k][...] = local_window[own, :] + arrived(2) + arrived(3)
         if k < 2:
             window[k, previous] = (local_window[previous, :] + arrived(0) + arrived(1)).astype(BF16)
-            window[k, own] = v[k].astype(BF16)
+            window[k, own] = basis[k][...].astype(BF16)
             window[k, following] = (local_window[following, :] + arrived(4) + arrived(5)).astype(
                 BF16
             )
 
-    keeps = [
-        pltpu.make_async_copy(v.at[k], out, keep_sem.at[k])
-        for k, out in enumerate((basis0_hbm, basis1_hbm, basis2_hbm))
-    ]
     send_contribs(0, picked)
 
     loads[7].wait()
@@ -378,8 +372,6 @@
             blocks[block]
         ].astype(BF16)
 
-    for i in reversed(used_routes(0)):
-        coarse_copy(i).start()
     high, low = two_parts(reach)
     corner_w[:, :CORNERS] = high
     corner_w[:, CORNERS:] = low
@@ -396,12 +388,16 @@
 
     lax.fori_loop(0, SLOTS // CASES, build_pick_t, 0)
     loads[8].wait()
+    for i in used_routes(0):
+        contrib_copy(0, i).wait_send()
+    for i in reversed(used_routes(0)):
+        coarse_copy(i).start()
     receive_contribs(0)
     for k in range(2):
         both = dot(corner_t[...], window[k])
         w_part[k] = both[:CORNERS] + both[CORNERS:]
         chip_copy(k).start()
-        norm = column_sum(v[k] * v[k])
+        norm = column_sum(basis[k][...] * basis[k][...])
         u = dot(pick_t[...], window[k]).astype(BF16)
         y = dot(dual[...], u)
         ring_sums = sum_rows(norm, column_sum(u.astype(F32) * y))
@@ -470,12 +466,10 @@
     alpha1 = norm1 / curve
     factor0[...] = alpha0 + alpha1 * grown
     factor1[...] = alpha0 * alpha1
-    for copy in keeps:
-        copy.wait()
     all_totals().wait_send()
 
     tail = near_copies() + [coarse_copy(i) for i in range(6)]
-    for k in range(3):
+    for k in range(1, 3):
         for i in used_routes(k):
             contrib_copy(k, i).wait_send()
     for k in range(2):
@@ -506,10 +500,10 @@
         v0, v1, v2, first, second = pl.pallas_call(
             functools.partial(kernel, spans, subs),
             name="creep_step",
-            out_shape=[jax.ShapeDtypeStruct((OWN, CASES), F32)] * 3
-            + [jax.ShapeDtypeStruct((1, CASES), F32)] * 2,
+            out_shape=[pltpu.VMEM((OWN, CASES), F32)] * 3
+            + [pltpu.VMEM((1, CASES), F32)] * 2,
             in_specs=[hbm] * 10,
-            out_specs=[hbm] * 3 + [vmem] * 2,
+            out_specs=[vmem] * 5,
             scratch_shapes=[
                 pltpu.SMEM((units,), F32),
                 pltpu.SMEM((units,), F32),
@@ -530,7 +524,6 @@
                 pltpu.VMEM((SLOTS, 2 * CASES), BF16),
                 pltpu.VMEM((2, SLOTS, CASES), BF16),
                 pltpu.VMEM((SLOTS, CASES), F32),
-                pltpu.VMEM((3, OWN, CASES), F32),
                 pltpu.VMEM((3, 3, OWN, CASES), CONTRIB),
                 pltpu.VMEM((3, 6, OWN, CASES), CONTRIB),
                 pltpu.VMEM((2, CORNERS, CASES), F32),
@@ -542,7 +535,6 @@
                 pltpu.VMEM((2, HALF + SUMS, CASES), F32),
                 pltpu.VMEM((spans, 4, CASES), F32),
                 dma((10,)),
-                dma((3,)),
                 dma((3, 6)),
                 dma((3, 6)),
                 dma((6,)),

time: 59.8 us -> 57.2 us (0.957)
  Pallas kernels: 56.6 us -> 55 us
  other arithmetic: 1.77 us -> 0.73 us
    pallas_call x1, Pallas kernels: 56.6 us -> 55 us  [on_device(): pl.pallas_call(functools.partial(kernel, spans, subs), name='creep_step',...]
    add x1, other arithmetic: 1.77 us -> 0.73 us  [on_device(): return (first * v0 - second * v1, v0 - first * v1 + second * v2)]
where the time goes in v6:
time: 57.2 us; the launch traced here: 57.1 us
  Pallas kernels  55 us (96%)
  between operations  1.29 us (2%)
  other arithmetic  0.73 us (1%)
    pallas_call x1, Pallas kernels, on_device(): pl.pallas_call(functools.partial(kernel, spans, subs), name='creep_step',...  55 us

profile of v6, /device:TPU:1, one launch (start us, length us, event | category | flops | bytes accessed | tf_op | source)
XLA Modules:
  0.0 57.1 jit_solution(9312674299079972247)
XLA Ops:
  1.3 55.0 %creep_step.1 = (f32[256,128]{1,0:T(8,128)S(1)}, f32[256,128]{1,0:T(8,128)S(1)}, f32[256,128]{1,0:T(8,128)S(1)}, f32[1,128]{1,0:T(1,128)S(1)}, f32[1,128]{1,0:T(1,128)S(1)}) custom-call(f32[8]{0:T(128)} %retard_hbm.1, f32[8]{0:T(128)} %compliance_hbm.1, s32[1,1]{1,0:T(1,128)} %bitcast.3.lengths_hbm, bf16[1,768,128]{2,1,0:T(8,128)(2,1)} %stress_hbm.1, ...), custom_call_target="tpu_custom_call" | custom-call | tf_op jit(solution)/shard_map/creep_step/pallas_call | solution.py:500
  56.3 0.7 %multiply_add_fusion = (f32[256,128]{1,0:T(8,128)}, f32[256,128]{1,0:T(8,128)}) fusion(f32[256,128]{1,0:T(8,128)S(1)} %get-tuple-element.11, f32[256,128]{1,0:T(8,128)S(1)} %get-tuple-element.8, f32[256,128]{1,0:T(8,128)S(1)} %get-tuple-element.10, f32[128]{0:T(128)S(1)} %bitcast.5, f32[128]{0:T(128)S(1)} %bitcast.4), kind=kLoop, calls=%fused_computation | loop fusion | flops 229376 | bytes 656384 | tf_op jit(solution)/shard_map/add | solution.py:564

commit v7 on v6

--- a/solution.py
+++ b/solution.py
@@ -37,11 +37,11 @@
     return jnp.transpose(jnp.broadcast_to(row, (CASES, SLOTS)))
 
 
-def sum_rows(first, second):
+def sum_rows(values):
     row = lax.broadcasted_iota(jnp.int32, (SUMS, CASES), 0)
     out = jnp.zeros((SUMS, CASES), F32)
-    for base, value in ((0, first), (3, second)):
-        rest = value
+    for number, value in enumerate(values):
+        base, rest = 3 * number, value
         for i in range(3):
             part = rest.astype(BF16).astype(F32)
             rest = rest - part
@@ -265,11 +265,13 @@
             device_id_type=MESH,
         )
 
+    ring_rows = (HALF, HALF + SUMS)
+
     def ring_copies(k):
         return [
             pltpu.make_async_remote_copy(
-                src_ref=ring_out.at[k],
-                dst_ref=ring_in.at[k, d - 1],
+                src_ref=ring_out.at[k, pl.ds(0, ring_rows[k])],
+                dst_ref=ring_in.at[k, d - 1, pl.ds(0, ring_rows[k])],
                 send_sem=ring_sem.at[k, 0],
                 recv_sem=ring_sem.at[k, 1],
                 device_id=(p, lax.rem(s + 2 * d, subs)),
@@ -280,8 +282,8 @@
 
     def all_ring(k):
         return pltpu.make_async_remote_copy(
-            src_ref=ring_in.at[k],
-            dst_ref=ring_in.at[k],
+            src_ref=ring_in.at[k, :, pl.ds(0, ring_rows[k])],
+            dst_ref=ring_in.at[k, :, pl.ds(0, ring_rows[k])],
             send_sem=ring_sem.at[k, 0],
             recv_sem=ring_sem.at[k, 1],
             device_id=partner,
@@ -290,8 +292,8 @@
 
     def pair_copy(k):
         return pltpu.make_async_remote_copy(
-            src_ref=pair_out.at[k],
-            dst_ref=pair_in.at[k],
+            src_ref=pair_out.at[k, pl.ds(0, ring_rows[k])],
+            dst_ref=pair_in.at[k, pl.ds(0, ring_rows[k])],
             send_sem=pair_sem.at[k, 0],
             recv_sem=pair_sem.at[k, 1],
             device_id=partner,
@@ -393,20 +395,30 @@
     for i in reversed(used_routes(0)):
         coarse_copy(i).start()
     receive_contribs(0)
+    products_so_far, energies = [], []
     for k in range(2):
         both = dot(corner_t[...], window[k])
         w_part[k] = both[:CORNERS] + both[CORNERS:]
         chip_copy(k).start()
-        norm = column_sum(basis[k][...] * basis[k][...])
         u = dot(pick_t[...], window[k]).astype(BF16)
-        y = dot(dual[...], u)
-        ring_sums = sum_rows(norm, column_sum(u.astype(F32) * y))
+
+        def products():
+            products_so_far.append(column_sum(basis[k][...] * basis[k][...]))
+            y = dot(dual[...], u)
+            products_so_far.append(column_sum(u.astype(F32) * y))
+            return y
+
+        if k == 1:
+            y = products()
+            ring_sums = sum_rows(products_so_far)
+            ring_out[k, HALF:] = ring_sums.astype(BF16)
         chip_copy(k).wait_recv()
         half = w_part[k, mine] + chip_in[k]
         ring_out[k, :HALF] = half.astype(BF16)
-        ring_out[k, HALF:] = ring_sums.astype(BF16)
         for copy in ring_copies(k):
             copy.start()
+        if k == 0:
+            y = products()
         high, low = two_parts(y)
         split[:, :CASES] = high
         split[:, CASES:] = low
@@ -418,9 +430,11 @@
         all_ring(k).wait_recv()
         for d in range(chips - 1):
             half = half + ring_in[k, d, :HALF].astype(F32)
-            ring_sums = ring_sums + ring_in[k, d, HALF:].astype(F32)
+            if k == 1:
+                ring_sums = ring_sums + ring_in[k, d, HALF:].astype(F32)
         pair_out[k, :HALF] = half
-        pair_out[k, HALF:] = ring_sums
+        if k == 1:
+            pair_out[k, HALF:] = ring_sums
         pair_copy(k).start()
         if k == 0:
             w_near[pl.ds(pl.multiple_of(2 * CORNERS + core * HALF, HALF), HALF), :] = half.astype(
@@ -435,7 +449,6 @@
             w_near[pl.ds(pl.multiple_of(3 * CORNERS - HALF - core * HALF, HALF), HALF), :] = pair_in[
                 k, :HALF
             ].astype(BF16)
-        ring_sums = ring_sums + pair_in[k, HALF:]
         w = w_full[...]
         z = jnp.dot(stiff[...], w, precision=lax.Precision.HIGHEST, preferred_element_type=F32)
         z_narrow = z.astype(BF16)
@@ -444,13 +457,14 @@
         def image(rows):
             return local_window[rows, :] + dot(corner_w[rows, :], z_twice)
 
+        energies.append(column_sum(w * z_narrow.astype(F32)))
         if k == 1:
+            ring_sums = ring_sums + pair_in[k, HALF:]
+            for i in range(4):
+                row = column_sum(ring_sums[3 * i : 3 * i + 3])
+                totals[0, i : i + 1] = row + energies[i // 2] if i % 2 else row
+            send_totals()
             send_contribs(2, image)
-        energy = column_sum(w * z_narrow.astype(F32))
-        totals[0, 2 * k : 2 * k + 1] = column_sum(ring_sums[0:3])
-        totals[0, 2 * k + 1 : 2 * k + 2] = column_sum(ring_sums[3:6]) + energy
-        if k == 1:
-            send_totals()
         if k == 1:
             local_window[own, :] = image(own)
         receive_contribs(k + 1)

time: 57.2 us -> 56.8 us (level)
  no operation moved by 1% of the time
where the time goes in v7:
time: 56.8 us; the launch traced here: 56.7 us
  Pallas kernels  54.7 us (96%)
  between operations  1.29 us (2%)
  other arithmetic  0.73 us (1%)
    pallas_call x1, Pallas kernels, on_device(): pl.pallas_call(functools.partial(kernel, spans, subs), name='creep_step',...  54.7 us

profile of v7, /device:TPU:1, one launch (start us, length us, event | category | flops | bytes accessed | tf_op | source)
XLA Modules:
  0.0 56.7 jit_solution(2722526782513671925)
XLA Ops:
  1.3 54.7 %creep_step.1 = (f32[256,128]{1,0:T(8,128)S(1)}, f32[256,128]{1,0:T(8,128)S(1)}, f32[256,128]{1,0:T(8,128)S(1)}, f32[1,128]{1,0:T(1,128)S(1)}, f32[1,128]{1,0:T(1,128)S(1)}) custom-call(f32[8]{0:T(128)} %retard_hbm.1, f32[8]{0:T(128)} %compliance_hbm.1, s32[1,1]{1,0:T(1,128)} %bitcast.3.lengths_hbm, bf16[1,768,128]{2,1,0:T(8,128)(2,1)} %stress_hbm.1, ...), custom_call_target="tpu_custom_call" | custom-call | tf_op jit(solution)/shard_map/creep_step/pallas_call | solution.py:514
  55.9 0.7 %multiply_add_fusion = (f32[256,128]{1,0:T(8,128)}, f32[256,128]{1,0:T(8,128)}) fusion(f32[256,128]{1,0:T(8,128)S(1)} %get-tuple-element.11, f32[256,128]{1,0:T(8,128)S(1)} %get-tuple-element.8, f32[256,128]{1,0:T(8,128)S(1)} %get-tuple-element.10, f32[128]{0:T(128)S(1)} %bitcast.5, f32[128]{0:T(128)S(1)} %bitcast.4), kind=kLoop, calls=%fused_computation | loop fusion | flops 229376 | bytes 656384 | tf_op jit(solution)/shard_map/add | solution.py:578

commit v8 on v7

--- a/solution.py
+++ b/solution.py
@@ -267,25 +267,28 @@
 
     ring_rows = (HALF, HALF + SUMS)
 
-    def ring_copies(k):
+    def ring_part(part):
+        return pl.ds(part * HALF, SUMS if part else HALF)
+
+    def ring_copies(k, part):
         return [
             pltpu.make_async_remote_copy(
-                src_ref=ring_out.at[k, pl.ds(0, ring_rows[k])],
-                dst_ref=ring_in.at[k, d - 1, pl.ds(0, ring_rows[k])],
-                send_sem=ring_sem.at[k, 0],
-                recv_sem=ring_sem.at[k, 1],
+                src_ref=ring_out.at[k, ring_part(part)],
+                dst_ref=ring_in.at[k, d - 1, ring_part(part)],
+                send_sem=ring_sem.at[k + part, 0],
+                recv_sem=ring_sem.at[k + part, 1],
                 device_id=(p, lax.rem(s + 2 * d, subs)),
                 device_id_type=MESH,
             )
             for d in sorted(range(1, chips), key=lambda d: -min(d, chips - d))
         ]
 
-    def all_ring(k):
+    def all_ring(k, part):
         return pltpu.make_async_remote_copy(
-            src_ref=ring_in.at[k, :, pl.ds(0, ring_rows[k])],
-            dst_ref=ring_in.at[k, :, pl.ds(0, ring_rows[k])],
-            send_sem=ring_sem.at[k, 0],
-            recv_sem=ring_sem.at[k, 1],
+            src_ref=ring_in.at[k, :, ring_part(part)],
+            dst_ref=ring_in.at[k, :, ring_part(part)],
+            send_sem=ring_sem.at[k + part, 0],
+            recv_sem=ring_sem.at[k + part, 1],
             device_id=partner,
             device_id_type=MESH,
         )
@@ -408,17 +411,17 @@
             products_so_far.append(column_sum(u.astype(F32) * y))
             return y
 
-        if k == 1:
-            y = products()
-            ring_sums = sum_rows(products_so_far)
-            ring_out[k, HALF:] = ring_sums.astype(BF16)
         chip_copy(k).wait_recv()
         half = w_part[k, mine] + chip_in[k]
         ring_out[k, :HALF] = half.astype(BF16)
-        for copy in ring_copies(k):
+        for copy in ring_copies(k, 0):
             copy.start()
-        if k == 0:
-            y = products()
+        y = products()
+        if k == 1:
+            ring_sums = sum_rows(products_so_far)
+            ring_out[k, HALF:] = ring_sums.astype(BF16)
+            for copy in ring_copies(k, 1):
+                copy.start()
         high, low = two_parts(y)
         split[:, :CASES] = high
         split[:, CASES:] = low
@@ -427,7 +430,8 @@
         else:
             for block in blocks:
                 local_window[block, :] = picked(block)
-        all_ring(k).wait_recv()
+        for part in range(k + 1):
+            all_ring(k, part).wait_recv()
         for d in range(chips - 1):
             half = half + ring_in[k, d, :HALF].astype(F32)
             if k == 1:
@@ -487,7 +491,7 @@
         for i in used_routes(k):
             contrib_copy(k, i).wait_send()
     for k in range(2):
-        for copy in [chip_copy(k), pair_copy(k), all_ring(k)] + (tail if k == 0 else []):
+        for copy in [chip_copy(k), pair_copy(k)] + [all_ring(k, i) for i in range(k + 1)] + (tail if k == 0 else []):
             copy.wait_send()
 
 
@@ -556,7 +560,7 @@
                 dma((8,)),
                 dma((2,)),
                 dma((2, 2)),
-                dma((2, 2)),
+                dma((3, 2)),
                 dma((2, 2)),
                 dma((2,)),
             ],

time: 56.8 us -> 57.9 us (1.019)
  Pallas kernels: 54.7 us -> 55.8 us
    pallas_call x1, Pallas kernels: 54.7 us -> 55.8 us  [on_device(): pl.pallas_call(functools.partial(kernel, spans, subs), name='creep_step',...]
where the time goes in v8:
time: 57.9 us; the launch traced here: 57.8 us
  Pallas kernels  55.8 us (96%)
  between operations  1.29 us (2%)
  other arithmetic  0.73 us (1%)
    pallas_call x1, Pallas kernels, on_device(): pl.pallas_call(functools.partial(kernel, spans, subs), name='creep_step',...  55.8 us

profile of v8, /device:TPU:1, one launch (start us, length us, event | category | flops | bytes accessed | tf_op | source)
XLA Modules:
  0.0 57.8 jit_solution(5666300434311982927)
XLA Ops:
  1.3 55.8 %creep_step.1 = (f32[256,128]{1,0:T(8,128)S(1)}, f32[256,128]{1,0:T(8,128)S(1)}, f32[256,128]{1,0:T(8,128)S(1)}, f32[1,128]{1,0:T(1,128)S(1)}, f32[1,128]{1,0:T(1,128)S(1)}) custom-call(f32[8]{0:T(128)} %retard_hbm.1, f32[8]{0:T(128)} %compliance_hbm.1, s32[1,1]{1,0:T(1,128)} %bitcast.3.lengths_hbm, bf16[1,768,128]{2,1,0:T(8,128)(2,1)} %stress_hbm.1, ...), custom_call_target="tpu_custom_call" | custom-call | tf_op jit(solution)/shard_map/creep_step/pallas_call | solution.py:518
  57.0 0.7 %multiply_add_fusion = (f32[256,128]{1,0:T(8,128)}, f32[256,128]{1,0:T(8,128)}) fusion(f32[256,128]{1,0:T(8,128)S(1)} %get-tuple-element.11, f32[256,128]{1,0:T(8,128)S(1)} %get-tuple-element.8, f32[256,128]{1,0:T(8,128)S(1)} %get-tuple-element.10, f32[128]{0:T(128)S(1)} %bitcast.5, f32[128]{0:T(128)S(1)} %bitcast.4), kind=kLoop, calls=%fused_computation | loop fusion | flops 229376 | bytes 656384 | tf_op jit(solution)/shard_map/add | solution.py:582

commit v9 on v7

--- a/solution.py
+++ b/solution.py
@@ -301,8 +301,8 @@
         )
 
     def send_totals():
-        def step(i, carry):
-            d = 1 + lax.rem(i + spans // 3, spans - 1)
+        def step(i):
+            d = 1 + (i + spans // 3) % (spans - 1)
             pltpu.make_async_remote_copy(
                 src_ref=totals.at[0],
                 dst_ref=totals.at[d],
@@ -311,9 +311,9 @@
                 device_id=(lax.rem(p + d, spans), s),
                 device_id_type=MESH,
             ).start()
-            return carry
-
-        lax.fori_loop(0, spans - 1, step, 0)
+
+        for i in range(spans - 1):
+            step(i)
 
     def all_totals():
         rest = totals.at[pl.ds(1, spans - 1)]

time: 56.8 us -> 56.6 us (level)
  no operation moved by 1% of the time
where the time goes in v9:
time: 56.6 us; the launch traced here: 56.5 us
  Pallas kernels  54.4 us (96%)
  between operations  1.29 us (2%)
  other arithmetic  0.73 us (1%)
    pallas_call x1, Pallas kernels, on_device(): pl.pallas_call(functools.partial(kernel, spans, subs), name='creep_step',...  54.4 us

profile of v9, /device:TPU:1, one launch (start us, length us, event | category | flops | bytes accessed | tf_op | source)
XLA Modules:
  0.0 56.5 jit_solution(17678655516592873894)
XLA Ops:
  1.3 54.4 %creep_step.1 = (f32[256,128]{1,0:T(8,128)S(1)}, f32[256,128]{1,0:T(8,128)S(1)}, f32[256,128]{1,0:T(8,128)S(1)}, f32[1,128]{1,0:T(1,128)S(1)}, f32[1,128]{1,0:T(1,128)S(1)}) custom-call(f32[8]{0:T(128)} %retard_hbm.1, f32[8]{0:T(128)} %compliance_hbm.1, s32[1,1]{1,0:T(1,128)} %bitcast.3.lengths_hbm, bf16[1,768,128]{2,1,0:T(8,128)(2,1)} %stress_hbm.1, ...), custom_call_target="tpu_custom_call" | custom-call | tf_op jit(solution)/shard_map/creep_step/pallas_call | solution.py:514
  55.7 0.7 %multiply_add_fusion = (f32[256,128]{1,0:T(8,128)}, f32[256,128]{1,0:T(8,128)}) fusion(f32[256,128]{1,0:T(8,128)S(1)} %get-tuple-element.11, f32[256,128]{1,0:T(8,128)S(1)} %get-tuple-element.8, f32[256,128]{1,0:T(8,128)S(1)} %get-tuple-element.10, f32[128]{0:T(128)S(1)} %bitcast.5, f32[128]{0:T(128)S(1)} %bitcast.4), kind=kLoop, calls=%fused_computation | loop fusion | flops 229376 | bytes 656384 | tf_op jit(solution)/shard_map/add | solution.py:578
